TPU v7x, 32 devices: a whole 2x2x4 slice. The times are simulated.
32 devices in a mesh: groups: 2 (over x), tensor: 8 (over z, y), section: 2 (over core).
Axes of the slice: x: 2, y: 2, z: 4, core: 2. Of those that a mesh axis runs over, the one named last changes fastest.
Arguments:
- hidden: bfloat16 [2, 768, 32768], P('section', 'groups', 'tensor'), parts along dimension 1, may hold values from -6 to 6
- down_weight: bfloat16 [2, 32768, 8192], P('section', 'tensor'), may hold values from -0.046875 to 0.046875
- stream: bfloat16 [2, 768, 8192], P('section', 'groups', 'tensor'), parts along dimension 1, may hold values from -36 to 36
- norm_gain: bfloat16 [2, 8192], P('section', 'tensor'), may hold values from 0.25 to 1.75
Outputs:
- new_stream: bfloat16 [2, 768, 8192], P('section', 'groups', 'tensor'), parts along dimension 1
- next_input: bfloat16 [2, 768, 8192], P('section', 'groups', 'tensor'), parts along dimension 1
There are 2 independent parts, one for each index of `groups`. A program takes and returns all parts, laid end to end along the dimension named above; an argument that names none is the same for every part. Nothing has to cross between parts.
All inputs are finite; a program needn't handle non-finite values.
Results may differ from a plain program's by a relative error of at most 0.0015.
Values may be sent and summed in bfloat16 or wider, within the bound.
No kernel may reach another device: no remote copies, remote signals or barrier semaphores. Data moves between devices by JAX's collectives and lax.ppermute only.
A program may use at most 192 MiB of HBM per device.

v0:
```python
import jax
import jax.numpy as jnp
from jax import lax
from jax.sharding import PartitionSpec as P


def from_behind(block, axis, distance):
    devices = range(lax.axis_size(axis))
    route = [((i - distance) % len(devices), i) for i in devices]
    return lax.ppermute(block, axis, route)


def per_device(hidden, down_weight, stream, norm_gain):
    full_width = down_weight.shape[2]
    hidden_rows = hidden[0]
    weight_rows = down_weight[0]
    shares = lax.psum_scatter(
        lax.dot_general(
            weight_rows, hidden_rows, (((0,), (1,)), ((), ())), preferred_element_type=jnp.float32
        ),
        "tensor",
        scatter_dimension=0,
        tiled=True,
    )
    updated = stream[0].astype(jnp.float32) + shares.T
    whole_rows = lax.all_gather(updated.astype(jnp.bfloat16), "tensor", axis=1, tiled=True).astype(
        updated.dtype
    )
    squares = jnp.sum(whole_rows * whole_rows, axis=1)
    inverse = lax.rsqrt(squares / full_width + 1e-05)
    normed = (updated * inverse[:, None] * norm_gain[0].astype(jnp.float32)[None, :]).astype(
        jnp.bfloat16
    )
    passed = from_behind(normed, "section", 1)
    return (updated.astype(jnp.bfloat16)[None], passed[None])


def solution(mesh):
    in_specs = (
        P("section", "groups", "tensor"),
        P("section", "tensor", None),
        P("section", "groups", "tensor"),
        P("section", "tensor"),
    )
    out_specs = (P("section", "groups", "tensor"), P("section", "groups", "tensor"))
    return jax.shard_map(
        per_device, mesh=mesh, in_specs=in_specs, out_specs=out_specs, check_vma=False
    )
```

profile of v0, /device:TPU:0, one launch (start us, length us, event | category | flops | bytes accessed | tf_op | source)
XLA Modules:
  0.0 380.7 jit_solution(14666123199853336712)
XLA Ops:
  7.2 0.0 copy-start
  7.2 0.0 reduce-scatter.2.cloned.1.call-start
  7.2 1.8 copy-done
  9.1 43.2 %fusion = f32[8192,384]{1,0:T(8,128)} fusion(bf16[1,4096,8192]{2,1,0:T(8,128)(2,1)} %param.5, bf16[1,384,4096]{2,1,0:T(8,128)(2,1)S(1)} %copy-done), kind=kOutput, calls=%fused_computation | convolution fusion | flops 25769803776 | bytes 82837504 | tf_op jit(solution)/shard_map/dot_general | solution.py:18
  52.3 0.0 reduce-scatter.2.cloned.1.call-update
  52.3 0.0 copy-start.3
  52.3 0.2 all-gather.2.cloned.1.call-start
  52.5 2.3 copy.6
  54.8 207.6 %reduce-scatter.2.cloned.1.call-done = f32[1024,384]{1,0:T(8,128)} async-done(((f32[8192,384]{1,0:T(8,128)}), f32[1024,384]{1,0:T(8,128)}) %reduce-scatter.2.cloned.1.call-update) | async-done | bytes 1572880 | tf_op jit(solution)/shard_map/reduce_scatter | solution.py:17
  262.5 2.6 fusion.3
  265.1 0.0 all-gather.2.cloned.1.call-update
  265.1 0.0 copy-done.3
  265.1 98.2 %all-gather.2.cloned.1.call-done = bf16[384,8192]{0,1:T(8,128)(2,1)} async-done(((bf16[384,1024]{0,1:T(8,128)(2,1)}), bf16[384,8192]{0,1:T(8,128)(2,1)}) %all-gather.2.cloned.1.call-update) | async-done | bytes 6291472 | tf_op jit(solution)/shard_map/all_gather | solution.py:26
  363.4 0.0 copy-start.1
  363.4 0.0 copy-start.2
  363.4 4.3 %multiply_reduce_fusion = f32[384]{0:T(512)S(1)} fusion(bf16[384,8192]{0,1:T(8,128)(2,1)} %all-gather.2.cloned.1.call-done), kind=kLoop, calls=%fused_computation.2 | loop fusion | flops 9436800 | bytes 6292992 | tf_op jit(solution)/shard_map/reduce_sum | solution.py:29
  367.7 0.0 copy-done.1
  367.7 0.0 copy-done.2
  367.8 1.1 multiply_convert_fusion
  368.9 0.0 collective-permute-start
  368.9 2.3 copy.7
  371.2 0.3 collective-permute-done
  371.5 2.3 copy.8
  (2 shorter events, 0.0 us)
Async XLA Ops:
  7.2 1.9 copy-start
  7.2 255.3 %reduce-scatter.2.cloned.1.call-start = ((), (), s32[]{:S(2)}) async-start(), calls=%async_computation.1 | async-start | bytes 14155776 | tf_op jit(solution)/shard_map/reduce_scatter | solution.py:17
  52.3 212.8 %copy-start.3 = (bf16[1,1024]{1,0:T(2,128)(2,1)S(1)}, bf16[1,1024]{1,0:T(2,128)(2,1)}, u32[]{:S(2)}) copy-start(bf16[1,1024]{1,0:T(2,128)(2,1)} %param.7) | copy-start | bytes 6148
  52.3 311.1 %all-gather.2.cloned.1.call-start = ((), (), s32[]{:S(2)}) async-start(), calls=%async_computation.2 | async-start | bytes 7077888 | tf_op jit(solution)/shard_map/all_gather | solution.py:26
  363.4 4.4 %copy-start.1 = (bf16[1,384,1024]{1,2,0:T(8,128)(2,1)S(1)}, bf16[1,384,1024]{1,2,0:T(8,128)(2,1)}, u32[]{:S(2)}) copy-start(bf16[1,384,1024]{1,2,0:T(8,128)(2,1)} %copy.6) | copy-start | bytes 2359300
  363.4 4.4 %copy-start.2 = (f32[1024,384]{1,0:T(8,128)S(1)}, f32[1024,384]{1,0:T(8,128)}, u32[]{:S(2)}) copy-start(f32[1024,384]{1,0:T(8,128)} %reduce-scatter.2.cloned.1.call-done) | copy-start | bytes 4718596
  368.9 2.6 collective-permute-start
Sparse Core Ops, SparseCore 0:
  52.4 210.0 reduce-scatter.1
  265.2 98.0 all-gather.1
where the time goes:
time: 381 us
  waiting for transfers between devices  306 us (80%)
  matrix products  43.2 us (11%)
  between operations  14.1 us (4%)
  local copies, waits for them, and re-layouts  8.72 us (2%)
  other arithmetic  8.14 us (2%)
    reduce_scatter x1, waiting for transfers between devices, per_device(): lax.psum_scatter(lax.dot_general(weight_rows, hidden_rows, (((0,), (1,)),...  208 us
    all_gather x1, waiting for transfers between devices, per_device(): lax.all_gather(updated.astype(jnp.bfloat16), 'tensor', axis=1, tiled=True)  98.2 us
    dot_general x1, matrix products, per_device(): lax.dot_general(weight_rows, hidden_rows, (((0,), (1,)), ((), ())), prefe...  43.2 us
    unnamed x11, local copies, waits for them, and re-layouts  8.72 us
  transfers between devices with their start and end apart: 3, of which 3 were waited for; matrix products, arithmetic and copies ran while one was open for 1% of the time, Pallas kernels for 0%

commit v1 on v0

v1 whole, which is shorter than its diff:
```python
import jax
import jax.numpy as jnp
from jax import lax
from jax.experimental import pallas as pl
from jax.experimental.pallas import tpu as pltpu
from jax.sharding import PartitionSpec as P

F32 = jnp.float32
WIRE = jnp.float16
TILE = 512


def matmul_kernel(order_ref, hidden_ref, weight_ref, out_ref):
    out_ref[0] = jnp.dot(hidden_ref[...], weight_ref[...], preferred_element_type=F32)


def chunk_products(hidden, weight, order, width):
    rows, depth = hidden.shape
    chunks = order.shape[0]
    tile = min(TILE, width)
    tiles = width // tile
    return pl.pallas_call(
        matmul_kernel,
        out_shape=jax.ShapeDtypeStruct((chunks, rows, width), F32),
        grid_spec=pltpu.PrefetchScalarGridSpec(
            num_scalar_prefetch=1,
            grid=(chunks, tiles),
            in_specs=[
                pl.BlockSpec((rows, depth), lambda c, j, order: (0, 0)),
                pl.BlockSpec((depth, tile), lambda c, j, order: (0, order[c] * tiles + j)),
            ],
            out_specs=pl.BlockSpec((1, rows, tile), lambda c, j, order: (c, 0, j)),
        ),
        compiler_params=pltpu.CompilerParams(vmem_limit_bytes=32 * 2**20),
        cost_estimate=pl.CostEstimate(
            flops=2 * rows * depth * width * chunks,
            bytes_accessed=2 * depth * width * chunks + 4 * rows * width * chunks,
            transcendentals=0,
        ),
        name="chunk_products",
    )(order, hidden, weight)


def send(block, pairs):
    return lax.ppermute(block, "tensor", pairs)


def reduce_line_of_four(hidden, weight, width):
    me = lax.axis_index("tensor")
    z, y = me // 2, me % 2
    upper = z >= 2
    outer = (z == 0) | (z == 3)
    toward = jnp.where(outer, jnp.array([3, 2, 1, 0]), jnp.array([3, 2, 0, 1]))
    places = jnp.where(upper, 3 - toward, toward)
    theirs = (2 * places + 1 - y).astype(jnp.int32)
    mine = (2 * places + y).astype(jnp.int32)

    across = [(t, t ^ 1) for t in range(8)]
    inward = [(0, 2), (1, 3), (6, 4), (7, 5)]
    middle = [(2, 4), (3, 5), (4, 2), (5, 3)]
    ends = [(t, t ^ 2) for t in range(8)]

    first = chunk_products(hidden, weight, theirs[:1], width)
    got = [send(first[0].astype(WIRE), across)]
    rest = chunk_products(hidden, weight, theirs[1:], width)
    got += [send(rest[i].astype(WIRE), across) for i in range(3)]
    own = chunk_products(hidden, weight, mine, width)

    def held(slot):
        return own[slot] + got[slot].astype(F32)

    sums = held(0)
    in_a = send(sums.astype(WIRE), inward)
    mid_a = send((sums + in_a.astype(F32)).astype(WIRE), middle)
    sums = held(1)
    in_b = send(sums.astype(WIRE), inward)
    mid_b = send((sums + in_b.astype(F32)).astype(WIRE), middle)
    last = send((held(2) + mid_a.astype(F32)).astype(WIRE), ends)
    return held(3) + last.astype(F32) + mid_b.astype(F32)


def per_device(hidden, down_weight, stream, norm_gain):
    count = lax.axis_size("tensor")
    full_width = down_weight.shape[2]
    width = full_width // count
    if count == 8:
        projected = reduce_line_of_four(hidden[0], down_weight[0], width)
    else:
        projected = lax.psum_scatter(
            jnp.dot(hidden[0], down_weight[0], preferred_element_type=F32),
            "tensor",
            scatter_dimension=1,
            tiled=True,
        )
    updated = stream[0].astype(F32) + projected
    swap = [(0, 1), (1, 0)]
    passed = lax.ppermute(updated * norm_gain[0].astype(F32)[None, :], "section", swap)
    squares = lax.ppermute(jnp.sum(updated * updated, axis=1), "section", swap)
    step = 1
    while step < count:
        squares = squares + send(squares, [(t, t ^ step) for t in range(count)])
        step *= 2
    inverse = lax.rsqrt(squares / full_width + 1e-05)
    normed = (passed * inverse[:, None]).astype(jnp.bfloat16)
    return (updated.astype(jnp.bfloat16)[None], normed[None])


def solution(mesh):
    in_specs = (
        P("section", "groups", "tensor"),
        P("section", "tensor", None),
        P("section", "groups", "tensor"),
        P("section", "tensor"),
    )
    out_specs = (P("section", "groups", "tensor"), P("section", "groups", "tensor"))
    return jax.shard_map(
        per_device, mesh=mesh, in_specs=in_specs, out_specs=out_specs, check_vma=False
    )
```

time: 381 us -> 132 us (0.35)
  waiting for transfers between devices: 306 us -> 55.1 us
  matrix products: 43.2 us -> 0 us
  Pallas kernels: 0 us -> 39.6 us
  starting transfers between devices: 0.26 us -> 25.5 us
  between operations: 14.1 us -> 0.82 us
  local copies, waits for them, and re-layouts: 8.72 us -> 3.77 us
    reduce_scatter x1 -> x0, waiting for transfers between devices: 208 us -> none  [per_device(): lax.psum_scatter(lax.dot_general(weight_rows, hidden_rows, (((0,), (1,)),...]
    all_gather x1 -> x0, waiting for transfers between devices: 98.2 us -> none  [per_device(): lax.all_gather(updated.astype(jnp.bfloat16), 'tensor', axis=1, tiled=True)]
    ppermute x1 -> x14, waiting for transfers between devices: 0.34 us -> 55.1 us  [the longest x12 52.2 us: send(): return lax.ppermute(block, 'tensor', pairs)]
    dot_general x1 -> x0, matrix products: 43.2 us -> none  [per_device(): lax.dot_general(weight_rows, hidden_rows, (((0,), (1,)), ((), ())), prefe...]
    pallas_call x0 -> x3, Pallas kernels: none -> 39.6 us  [chunk_products(): pl.pallas_call(matmul_kernel, out_shape=jax.ShapeDtypeStruct((chunks, row...]
    ppermute x1 -> x14, starting transfers between devices: 0.01 us -> 25.5 us  [the longest x12 25 us: send(): return lax.ppermute(block, 'tensor', pairs)]
    unnamed x11 -> x8, local copies, waits for them, and re-layouts: 8.72 us -> 3.05 us
  transfers between devices with their start and end apart: 3 -> 14, of which waited for: 3 -> 7; matrix products, arithmetic and copies ran while one was open for 1% -> 3% of each run, Pallas kernels for 0% -> 26%
where the time goes in v1:
time: 132 us; the launch traced here: 131 us
  waiting for transfers between devices  55.1 us (42%)
  Pallas kernels  39.6 us (30%)
  starting transfers between devices  25.5 us (19%)
  other arithmetic  6.24 us (5%)
  local copies, waits for them, and re-layouts  3.77 us (3%)
    ppermute x12, waiting for transfers between devices, send(): return lax.ppermute(block, 'tensor', pairs)  52.2 us
    pallas_call x3, Pallas kernels, chunk_products(): pl.pallas_call(matmul_kernel, out_shape=jax.ShapeDtypeStruct((chunks, row...  39.6 us
    ppermute x12, starting transfers between devices, send(): return lax.ppermute(block, 'tensor', pairs)  25 us
    unnamed x8, local copies, waits for them, and re-layouts  3.05 us
    ppermute x1, waiting for transfers between devices, per_device(): squares = lax.ppermute(jnp.sum(updated * updated, axis=1), 'section', swap)  2.9 us
  transfers between devices with their start and end apart: 14, of which 7 were waited for; matrix products, arithmetic and copies ran while one was open for 3% of the time, Pallas kernels for 26%

profile of v1, /device:TPU:0, one launch (start us, length us, event | category | flops | bytes accessed | tf_op | source)
XLA Modules:
  0.0 131.0 jit_solution(13342920178414859550)
XLA Ops:
  0.7 0.7 broadcast_add_fusion
  1.3 0.0 copy-start
  1.3 1.9 %copy-done = bf16[1,384,4096]{2,1,0:T(8,128)(2,1)S(1)} copy-done((bf16[1,384,4096]{2,1,0:T(8,128)(2,1)S(1)}, bf16[1,384,4096]{2,1,0:T(8,128)(2,1)}, u32[]{:S(2)}) %copy-start) | copy-done | bytes 3145752
  3.2 5.9 %chunk_products.5 = f32[1,384,1024]{2,1,0:T(8,128)S(1)} custom-call(s32[1]{0:T(128)S(1)} %bitcast.58, bf16[384,4096]{1,0:T(8,128)(2,1)S(1)} %bitcast.55, bf16[4096,8192]{1,0:T(8,128)(2,1)} %bitcast.2.weight_ref), custom_call_target="tpu_custom_call" | custom-call | flops 3221225472 | bytes 9961472 | tf_op jit(solution)/shard_map/chunk_products/pallas_call | solution.py:22
  9.1 0.1 convert_bitcast_fusion.1
  9.3 3.0 %collective-permute-start.2 = (f16[384,1024]{1,0:T(8,128)(2,1)S(1)}, f16[384,1024]{1,0:T(8,128)(2,1)S(1)}, u32[]{:S(2)}, u32[]{:S(2)}) collective-permute-start(f16[384,1024]{1,0:T(8,128)(2,1)S(1)} %convert_bitcast_fusion.1), channel_id=1, source_target_pairs={{0,2},{2,0},{4,6},{6,4},{8,10},{10,8},{12,14},{14,12},{1,3},{3,1},... | collective-permute-start | bytes 2359304 | tf_op jit(solution)/shard_map/ppermute | solution.py:45
  12.3 0.1 slice.31.order_ref
  12.4 14.6 %chunk_products.4 = f32[3,384,1024]{2,1,0:T(8,128)S(1)} custom-call(s32[3]{0:T(128)S(1)} %slice.31.order_ref, bf16[384,4096]{1,0:T(8,128)(2,1)S(1)} %bitcast.56, bf16[4096,8192]{1,0:T(8,128)(2,1)} %bitcast.2.weight_ref), custom_call_target="tpu_custom_call" | custom-call | flops 9663676416 | bytes 29884416 | tf_op jit(solution)/shard_map/chunk_products/pallas_call | solution.py:22
  27.0 0.5 convert.7
  27.5 0.0 copy-start.1
  27.6 0.6 slice_bitcast_fusion.6
  28.2 0.1 collective-permute-start.6
  28.3 1.1 copy-done.1
  29.4 19.0 %chunk_products.3 = f32[4,384,1024]{2,1,0:T(8,128)S(1)} custom-call(s32[4]{0:T(128)S(1)} %get-tuple-element.13.order_ref, bf16[384,4096]{1,0:T(8,128)(2,1)S(1)} %bitcast.57, bf16[4096,8192]{1,0:T(8,128)(2,1)} %bitcast.2.weight_ref), custom_call_target="tpu_custom_call" | custom-call | flops 12884901888 | bytes 39845888 | tf_op jit(solution)/shard_map/chunk_products/pallas_call | solution.py:22
  48.4 0.0 collective-permute-done.2
  48.4 0.3 fusion.9
  48.8 3.5 %collective-permute-start.3 = (f16[384,1024]{1,0:T(8,128)(2,1)S(1)}, f16[384,1024]{1,0:T(8,128)(2,1)S(1)}, u32[]{:S(2)}, u32[]{:S(2)}) collective-permute-start(f16[384,1024]{1,0:T(8,128)(2,1)S(1)} %fusion.9), channel_id=1, source_target_pairs={{0,4},{2,6},{12,8},{14,10},{1,5},{3,7},{13,9},{15,11},{16,20},{18,... | collective-permute-start | bytes 2359304 | tf_op jit(solution)/shard_map/ppermute | solution.py:45
  52.3 0.9 collective-permute-start.1
  53.2 0.0 collective-permute-done.6
  53.2 15.5 %collective-permute-done.3 = f16[384,1024]{1,0:T(8,128)(2,1)S(1)} collective-permute-done((f16[384,1024]{1,0:T(8,128)(2,1)S(1)}, f16[384,1024]{1,0:T(8,128)(2,1)S(1)}, u32[]{:S(2)}, u32[]{:S(2)}) %collective-permute-start.3) | collective-permute-done | bytes 786464 | tf_op jit(solution)/shard_map/ppermute | solution.py:45
  68.7 0.8 add_convert_fusion.1
  69.6 0.7 collective-permute-start.4
  70.3 7.2 %collective-permute-start.7 = (f16[384,1024]{1,0:T(8,128)(2,1)S(1)}, f16[384,1024]{1,0:T(8,128)(2,1)S(1)}, u32[]{:S(2)}, u32[]{:S(2)}) collective-permute-start(f16[384,1024]{1,0:T(8,128)(2,1)S(1)} %get-tuple-element.7), channel_id=1, source_target_pairs={{0,4},{2,6},{12,8},{14,10},{1,5},{3,7},{13,9},{15,11},{16,20},{18,... | collective-permute-start | bytes 2359304 | tf_op jit(solution)/shard_map/ppermute | solution.py:45
  77.5 0.0 copy-start.3
  77.5 0.0 copy-start.2
  77.5 0.7 collective-permute-start
  78.2 0.0 collective-permute-done.1
  78.2 0.0 collective-permute-done.4
  78.2 14.6 %collective-permute-done.7 = f16[384,1024]{1,0:T(8,128)(2,1)S(1)} collective-permute-done((f16[384,1024]{1,0:T(8,128)(2,1)S(1)}, f16[384,1024]{1,0:T(8,128)(2,1)S(1)}, u32[]{:S(2)}, u32[]{:S(2)}) %collective-permute-start.7) | collective-permute-done | bytes 786464 | tf_op jit(solution)/shard_map/ppermute | solution.py:45
  92.8 0.9 fusion.4
  93.7 2.5 %collective-permute-start.5 = (f16[384,1024]{1,0:T(8,128)(2,1)S(1)}, f16[384,1024]{1,0:T(8,128)(2,1)S(1)}, u32[]{:S(2)}, u32[]{:S(2)}) collective-permute-start(f16[384,1024]{1,0:T(8,128)(2,1)S(1)} %get-tuple-element.4), channel_id=1, source_target_pairs={{0,4},{2,6},{4,0},{6,2},{8,12},{10,14},{12,8},{14,10},{1,5},{3,7},... | collective-permute-start | bytes 2359304 | tf_op jit(solution)/shard_map/ppermute | solution.py:45
  96.3 0.7 collective-permute-start.8
  97.0 0.0 copy-done.3
  97.0 0.0 collective-permute-done
  97.0 14.4 %collective-permute-done.5 = f16[384,1024]{1,0:T(8,128)(2,1)S(1)} collective-permute-done((f16[384,1024]{1,0:T(8,128)(2,1)S(1)}, f16[384,1024]{1,0:T(8,128)(2,1)S(1)}, u32[]{:S(2)}, u32[]{:S(2)}) %collective-permute-start.5) | collective-permute-done | bytes 786464 | tf_op jit(solution)/shard_map/ppermute | solution.py:45
  111.4 0.0 collective-permute-done.8
  111.4 0.0 copy-done.2
  111.4 0.7 multiply_reduce_fusion
  112.1 1.1 broadcast_multiply_fusion
  113.2 0.0 collective-permute-start.9
  113.2 0.5 collective-permute-start.10
  113.7 2.9 %collective-permute-done.10 = f32[384]{0:T(512)S(1)} collective-permute-done((f32[384]{0:T(512)S(1)}, f32[384]{0:T(512)S(1)}, u32[]{:S(2)}, u32[]{:S(2)}) %collective-permute-start.10) | collective-permute-done | bytes 1568 | tf_op jit(solution)/shard_map/ppermute | solution.py:98
  116.6 0.0 collective-permute-start.11
  116.7 3.6 %collective-permute-done.11 = f32[384]{0:T(512)S(1)} collective-permute-done((f32[384]{0:T(512)S(1)}, f32[384]{0:T(512)S(1)}, u32[]{:S(2)}, u32[]{:S(2)}) %collective-permute-start.11) | collective-permute-done | bytes 1568 | tf_op jit(solution)/shard_map/ppermute | solution.py:45
  120.2 3.6 %collective-permute-start.12 = (f32[384]{0:T(512)S(1)}, f32[384]{0:T(512)S(1)}, u32[]{:S(2)}, u32[]{:S(2)}) collective-permute-start(f32[384]{0:T(512)S(1)} %add.73), channel_id=1, source_target_pairs={{0,4},{2,6},{4,0},{6,2},{8,12},{10,14},{12,8},{14,10},{1,5},{3,7},... | collective-permute-start | bytes 4616 | tf_op jit(solution)/shard_map/ppermute | solution.py:45
  123.9 1.6 %collective-permute-done.12 = f32[384]{0:T(512)S(1)} collective-permute-done((f32[384]{0:T(512)S(1)}, f32[384]{0:T(512)S(1)}, u32[]{:S(2)}, u32[]{:S(2)}) %collective-permute-start.12) | collective-permute-done | bytes 1568 | tf_op jit(solution)/shard_map/ppermute | solution.py:45
  125.4 1.9 %collective-permute-start.13 = (f32[384]{0:T(512)S(1)}, f32[384]{0:T(512)S(1)}, u32[]{:S(2)}, u32[]{:S(2)}) collective-permute-start(f32[384]{0:T(512)S(1)} %add.74), channel_id=1, source_target_pairs={{0,8},{2,10},{4,12},{6,14},{8,0},{10,2},{12,4},{14,6},{1,9},{3,11}... | collective-permute-start | bytes 4616 | tf_op jit(solution)/shard_map/ppermute | solution.py:45
  127.4 2.6 %collective-permute-done.13 = f32[384]{0:T(512)S(1)} collective-permute-done((f32[384]{0:T(512)S(1)}, f32[384]{0:T(512)S(1)}, u32[]{:S(2)}, u32[]{:S(2)}) %collective-permute-start.13) | collective-permute-done | bytes 1568 | tf_op jit(solution)/shard_map/ppermute | solution.py:45
  129.9 0.0 collective-permute-done.9
  129.9 1.0 fusion.11
  (4 shorter events, 0.0 us)
Async XLA Ops:
  1.3 1.9 %copy-start = (bf16[1,384,4096]{2,1,0:T(8,128)(2,1)S(1)}, bf16[1,384,4096]{2,1,0:T(8,128)(2,1)}, u32[]{:S(2)}) copy-start(bf16[1,384,4096]{2,1,0:T(8,128)(2,1)} %param.6) | copy-start | bytes 9437188
  9.3 39.2 %collective-permute-start.2 = (f16[384,1024]{1,0:T(8,128)(2,1)S(1)}, f16[384,1024]{1,0:T(8,128)(2,1)S(1)}, u32[]{:S(2)}, u32[]{:S(2)}) collective-permute-start(f16[384,1024]{1,0:T(8,128)(2,1)S(1)} %convert_bitcast_fusion.1), channel_id=1, source_target_pairs={{0,2},{2,0},{4,6},{6,4},{8,10},{10,8},{12,14},{14,12},{1,3},{3,1},... | collective-permute-start | bytes 2359304 | tf_op jit(solution)/shard_map/ppermute | solution.py:45
  27.5 1.9 %copy-start.1 = (bf16[1,384,4096]{2,1,0:T(8,128)(2,1)S(1)}, bf16[1,384,4096]{2,1,0:T(8,128)(2,1)}, u32[]{:S(2)}) copy-start(bf16[1,384,4096]{2,1,0:T(8,128)(2,1)} %param.6) | copy-start | bytes 9437188
  28.2 25.0 %collective-permute-start.6 = (f16[384,1024]{1,0:T(8,128)(2,1)S(1)}, f16[384,1024]{1,0:T(8,128)(2,1)S(1)}, u32[]{:S(2)}, u32[]{:S(2)}) collective-permute-start(f16[384,1024]{1,0:T(8,128)(2,1)S(1)} %get-tuple-element.9), channel_id=1, source_target_pairs={{0,2},{2,0},{4,6},{6,4},{8,10},{10,8},{12,14},{14,12},{1,3},{3,1},... | collective-permute-start | bytes 2359304 | tf_op jit(solution)/shard_map/ppermute | solution.py:45
  48.8 20.0 %collective-permute-start.3 = (f16[384,1024]{1,0:T(8,128)(2,1)S(1)}, f16[384,1024]{1,0:T(8,128)(2,1)S(1)}, u32[]{:S(2)}, u32[]{:S(2)}) collective-permute-start(f16[384,1024]{1,0:T(8,128)(2,1)S(1)} %fusion.9), channel_id=1, source_target_pairs={{0,4},{2,6},{12,8},{14,10},{1,5},{3,7},{13,9},{15,11},{16,20},{18,... | collective-permute-start | bytes 2359304 | tf_op jit(solution)/shard_map/ppermute | solution.py:45
  52.3 25.9 %collective-permute-start.1 = (f16[384,1024]{1,0:T(8,128)(2,1)S(1)}, f16[384,1024]{1,0:T(8,128)(2,1)S(1)}, u32[]{:S(2)}, u32[]{:S(2)}) collective-permute-start(f16[384,1024]{1,0:T(8,128)(2,1)S(1)} %get-tuple-element.10), channel_id=1, source_target_pairs={{0,2},{2,0},{4,6},{6,4},{8,10},{10,8},{12,14},{14,12},{1,3},{3,1},... | collective-permute-start | bytes 2359304 | tf_op jit(solution)/shard_map/ppermute | solution.py:45
  69.6 8.6 %collective-permute-start.4 = (f16[384,1024]{1,0:T(8,128)(2,1)S(1)}, f16[384,1024]{1,0:T(8,128)(2,1)S(1)}, u32[]{:S(2)}, u32[]{:S(2)}) collective-permute-start(f16[384,1024]{1,0:T(8,128)(2,1)S(1)} %get-tuple-element.6), channel_id=1, source_target_pairs={{4,8},{6,10},{8,4},{10,6},{5,9},{7,11},{9,5},{11,7},{20,24},{22,26... | collective-permute-start | bytes 2359304 | tf_op jit(solution)/shard_map/ppermute | solution.py:45
  70.3 22.5 %collective-permute-start.7 = (f16[384,1024]{1,0:T(8,128)(2,1)S(1)}, f16[384,1024]{1,0:T(8,128)(2,1)S(1)}, u32[]{:S(2)}, u32[]{:S(2)}) collective-permute-start(f16[384,1024]{1,0:T(8,128)(2,1)S(1)} %get-tuple-element.7), channel_id=1, source_target_pairs={{0,4},{2,6},{12,8},{14,10},{1,5},{3,7},{13,9},{15,11},{16,20},{18,... | collective-permute-start | bytes 2359304 | tf_op jit(solution)/shard_map/ppermute | solution.py:45
  77.5 19.5 %copy-start.3 = (bf16[1,1024]{1,0:T(2,128)(2,1)S(1)}, bf16[1,1024]{1,0:T(2,128)(2,1)}, u32[]{:S(2)}) copy-start(bf16[1,1024]{1,0:T(2,128)(2,1)} %param.9) | copy-start | bytes 6148
  77.5 33.9 %copy-start.2 = (bf16[1,384,1024]{2,1,0:T(8,128)(2,1)S(1)}, bf16[1,384,1024]{2,1,0:T(8,128)(2,1)}, u32[]{:S(2)}) copy-start(bf16[1,384,1024]{2,1,0:T(8,128)(2,1)} %param.8) | copy-start | bytes 2359300
  77.5 19.5 %collective-permute-start = (f16[384,1024]{1,0:T(8,128)(2,1)S(1)}, f16[384,1024]{1,0:T(8,128)(2,1)S(1)}, u32[]{:S(2)}, u32[]{:S(2)}) collective-permute-start(f16[384,1024]{1,0:T(8,128)(2,1)S(1)} %get-tuple-element.8), channel_id=1, source_target_pairs={{0,2},{2,0},{4,6},{6,4},{8,10},{10,8},{12,14},{14,12},{1,3},{3,1},... | collective-permute-start | bytes 2359304 | tf_op jit(solution)/shard_map/ppermute | solution.py:45
  93.7 17.7 %collective-permute-start.5 = (f16[384,1024]{1,0:T(8,128)(2,1)S(1)}, f16[384,1024]{1,0:T(8,128)(2,1)S(1)}, u32[]{:S(2)}, u32[]{:S(2)}) collective-permute-start(f16[384,1024]{1,0:T(8,128)(2,1)S(1)} %get-tuple-element.4), channel_id=1, source_target_pairs={{0,4},{2,6},{4,0},{6,2},{8,12},{10,14},{12,8},{14,10},{1,5},{3,7},... | collective-permute-start | bytes 2359304 | tf_op jit(solution)/shard_map/ppermute | solution.py:45
  96.3 15.1 %collective-permute-start.8 = (f16[384,1024]{1,0:T(8,128)(2,1)S(1)}, f16[384,1024]{1,0:T(8,128)(2,1)S(1)}, u32[]{:S(2)}, u32[]{:S(2)}) collective-permute-start(f16[384,1024]{1,0:T(8,128)(2,1)S(1)} %get-tuple-element.5), channel_id=1, source_target_pairs={{4,8},{6,10},{8,4},{10,6},{5,9},{7,11},{9,5},{11,7},{20,24},{22,26... | collective-permute-start | bytes 2359304 | tf_op jit(solution)/shard_map/ppermute | solution.py:45
  113.2 16.7 %collective-permute-start.9 = (f32[384,1024]{1,0:T(8,128)S(1)}, f32[384,1024]{1,0:T(8,128)S(1)}, u32[]{:S(2)}, u32[]{:S(2)}) collective-permute-start(f32[384,1024]{1,0:T(8,128)S(1)} %get-tuple-element.11), channel_id=1, source_target_pairs={{0,1},{1,0},{2,3},{3,2},{4,5},{5,4},{6,7},{7,6},{8,9},{9,8},{10,11... | collective-permute-start | bytes 4718600 | tf_op jit(solution)/shard_map/ppermute | solution.py:97
  113.2 3.4 %collective-permute-start.10 = (f32[384]{0:T(512)S(1)}, f32[384]{0:T(512)S(1)}, u32[]{:S(2)}, u32[]{:S(2)}) collective-permute-start(f32[384]{0:T(512)S(1)} %get-tuple-element.2), channel_id=1, source_target_pairs={{0,1},{1,0},{2,3},{3,2},{4,5},{5,4},{6,7},{7,6},{8,9},{9,8},{10,11... | collective-permute-start | bytes 4616 | tf_op jit(solution)/shard_map/ppermute | solution.py:98
  116.6 3.6 %collective-permute-start.11 = (f32[384]{0:T(512)S(1)}, f32[384]{0:T(512)S(1)}, u32[]{:S(2)}, u32[]{:S(2)}) collective-permute-start(f32[384]{0:T(512)S(1)} %collective-permute-done.10), channel_id=1, source_target_pairs={{0,2},{2,0},{4,6},{6,4},{8,10},{10,8},{12,14},{14,12},{1,3},{3,1},... | collective-permute-start | bytes 4616 | tf_op jit(solution)/shard_map/ppermute | solution.py:45
  120.2 5.2 %collective-permute-start.12 = (f32[384]{0:T(512)S(1)}, f32[384]{0:T(512)S(1)}, u32[]{:S(2)}, u32[]{:S(2)}) collective-permute-start(f32[384]{0:T(512)S(1)} %add.73), channel_id=1, source_target_pairs={{0,4},{2,6},{4,0},{6,2},{8,12},{10,14},{12,8},{14,10},{1,5},{3,7},... | collective-permute-start | bytes 4616 | tf_op jit(solution)/shard_map/ppermute | solution.py:45
  125.4 4.5 %collective-permute-start.13 = (f32[384]{0:T(512)S(1)}, f32[384]{0:T(512)S(1)}, u32[]{:S(2)}, u32[]{:S(2)}) collective-permute-start(f32[384]{0:T(512)S(1)} %add.74), channel_id=1, source_target_pairs={{0,8},{2,10},{4,12},{6,14},{8,0},{10,2},{12,4},{14,6},{1,9},{3,11}... | collective-permute-start | bytes 4616 | tf_op jit(solution)/shard_map/ppermute | solution.py:45

commit v2 on v1

--- a/solution.py
+++ b/solution.py
@@ -60,11 +60,21 @@
     middle = [(2, 4), (3, 5), (4, 2), (5, 3)]
     ends = [(t, t ^ 2) for t in range(8)]
 
+    def both(indices):
+        return chunk_products(hidden, weight, jnp.concatenate(indices), width)
+
+    def cross(block):
+        return send(block.astype(WIRE), across)
+
     first = chunk_products(hidden, weight, theirs[:1], width)
-    got = [send(first[0].astype(WIRE), across)]
-    rest = chunk_products(hidden, weight, theirs[1:], width)
-    got += [send(rest[i].astype(WIRE), across) for i in range(3)]
-    own = chunk_products(hidden, weight, mine, width)
+    got = [cross(first[0])]
+    second = both((theirs[1:2], mine[:1]))
+    got.append(cross(second[0]))
+    third = both((theirs[2:3], mine[1:2]))
+    got.append(cross(third[0]))
+    fourth = both((theirs[3:], mine[2:]))
+    got.append(cross(fourth[0]))
+    own = [second[1], third[1], fourth[1], fourth[2]]
 
     def held(slot):
         return own[slot] + got[slot].astype(F32)
@@ -77,6 +87,23 @@
     mid_b = send((sums + in_b.astype(F32)).astype(WIRE), middle)
     last = send((held(2) + mid_a.astype(F32)).astype(WIRE), ends)
     return held(3) + last.astype(F32) + mid_b.astype(F32)
+
+
+def total_squares(squares, count):
+    swap = [(0, 1), (1, 0)]
+    if count != 8:
+        squares = lax.ppermute(squares, "section", swap)
+        step = 1
+        while step < count:
+            squares = squares + send(squares, [(t, t ^ step) for t in range(count)])
+            step *= 2
+        return squares
+    corner = [(2 * t + s, 2 * (t ^ 1) + 1 - s) for t in range(8) for s in range(2)]
+    squares = lax.ppermute(squares, "section", swap) + lax.ppermute(
+        squares, ("tensor", "section"), corner
+    )
+    others = [send(squares, [(t, t ^ step) for t in range(8)]) for step in (2, 4, 6)]
+    return squares + others[0] + (others[1] + others[2])
 
 
 def per_device(hidden, down_weight, stream, norm_gain):
@@ -93,13 +120,9 @@
             tiled=True,
         )
     updated = stream[0].astype(F32) + projected
-    swap = [(0, 1), (1, 0)]
-    passed = lax.ppermute(updated * norm_gain[0].astype(F32)[None, :], "section", swap)
-    squares = lax.ppermute(jnp.sum(updated * updated, axis=1), "section", swap)
-    step = 1
-    while step < count:
-        squares = squares + send(squares, [(t, t ^ step) for t in range(count)])
-        step *= 2
+    squares = total_squares(jnp.sum(updated * updated, axis=1), count)
+    scaled = updated * norm_gain[0].astype(F32)[None, :]
+    passed = lax.ppermute(scaled, "section", [(0, 1), (1, 0)])
     inverse = lax.rsqrt(squares / full_width + 1e-05)
     normed = (passed * inverse[:, None]).astype(jnp.bfloat16)
     return (updated.astype(jnp.bfloat16)[None], normed[None])

time: 132 us -> 105 us (0.80)
  waiting for transfers between devices: 55.1 us -> 24 us
  Pallas kernels: 39.6 us -> 43.1 us
  other arithmetic: 6.24 us -> 9.19 us
    ppermute x12, waiting for transfers between devices: 52.2 us -> 21.1 us  [send(): return lax.ppermute(block, 'tensor', pairs)]
    pallas_call x3 -> x4, Pallas kernels: 39.6 us -> 43.1 us  [chunk_products(): pl.pallas_call(matmul_kernel, out_shape=jax.ShapeDtypeStruct((chunks, row...]
    concatenate x0 -> x3, other arithmetic: none -> 3.3 us  [both(): return chunk_products(hidden, weight, jnp.concatenate(indices), width)]
    ppermute x2 -> x3, waiting for transfers between devices: 2.9 us -> 2.8 us  [the longest x1 2.4 us: total_squares(): lax.ppermute(squares, ('tensor', 'section'), corner)]
  transfers between devices with their start and end apart: 14 -> 15, of which waited for: 7 -> 7; matrix products, arithmetic and copies ran while one was open for 3% -> 5% of each run, Pallas kernels for 26% -> 35%
where the time goes in v2:
time: 105 us
  Pallas kernels  43.1 us (41%)
  starting transfers between devices  25.1 us (24%)
  waiting for transfers between devices  24 us (23%)
  other arithmetic  9.19 us (9%)
  local copies, waits for them, and re-layouts  2.64 us (3%)
    pallas_call x4, Pallas kernels, chunk_products(): pl.pallas_call(matmul_kernel, out_shape=jax.ShapeDtypeStruct((chunks, row...  43.1 us
    ppermute x12, starting transfers between devices, send(): return lax.ppermute(block, 'tensor', pairs)  24.4 us
    ppermute x12, waiting for transfers between devices, send(): return lax.ppermute(block, 'tensor', pairs)  21.1 us
    concatenate x3, other arithmetic, both(): return chunk_products(hidden, weight, jnp.concatenate(indices), width)  3.3 us
    ppermute x1, waiting for transfers between devices, total_squares(): lax.ppermute(squares, ('tensor', 'section'), corner)  2.4 us
  transfers between devices with their start and end apart: 15, of which 7 were waited for; matrix products, arithmetic and copies ran while one was open for 5% of the time, Pallas kernels for 35%

profile of v2, /device:TPU:0, one launch (start us, length us, event | category | flops | bytes accessed | tf_op | source)
XLA Modules:
  0.0 104.8 jit_solution(9995073907300924161)
XLA Ops:
  0.7 0.7 add_subtract_fusion
  1.3 0.7 fusion.17
  2.0 0.0 copy-start
  2.0 1.9 %copy-done = bf16[1,384,4096]{2,1,0:T(8,128)(2,1)S(1)} copy-done((bf16[1,384,4096]{2,1,0:T(8,128)(2,1)S(1)}, bf16[1,384,4096]{2,1,0:T(8,128)(2,1)}, u32[]{:S(2)}) %copy-start) | copy-done | bytes 3145752
  3.9 0.0 copy-start.1
  3.9 6.8 %chunk_products.7 = f32[1,384,1024]{2,1,0:T(8,128)S(1)} custom-call(s32[1]{0:T(128)} %get-tuple-element.8.order_ref, bf16[384,4096]{1,0:T(8,128)(2,1)S(1)} %bitcast.54, bf16[4096,8192]{1,0:T(8,128)(2,1)} %bitcast.2.weight_ref), custom_call_target="tpu_custom_call" | custom-call | flops 3221225472 | bytes 9961472 | tf_op jit(solution)/shard_map/chunk_products/pallas_call | solution.py:22
  10.7 0.1 convert_bitcast_fusion.1
  10.8 3.0 %collective-permute-start.2 = (f16[384,1024]{1,0:T(8,128)(2,1)S(1)}, f16[384,1024]{1,0:T(8,128)(2,1)S(1)}, u32[]{:S(2)}, u32[]{:S(2)}) collective-permute-start(f16[384,1024]{1,0:T(8,128)(2,1)S(1)} %convert_bitcast_fusion.1), channel_id=1, source_target_pairs={{0,2},{2,0},{4,6},{6,4},{8,10},{10,8},{12,14},{14,12},{1,3},{3,1},... | collective-permute-start | bytes 2359304 | tf_op jit(solution)/shard_map/ppermute | solution.py:45
  13.9 1.3 %pad_add_fusion.2.order_ref = s32[2]{0:T(128)S(1)} fusion(s32[1]{0:T(128)} %get-tuple-element.14, s32[1]{0:T(128)} %get-tuple-element.9), kind=kLoop, calls=%fused_computation.35 | loop fusion | flops 2 | bytes 16 | tf_op jit(solution)/shard_map/concatenate | solution.py:64
  15.2 0.0 copy-done.1
  15.2 10.7 %chunk_products.6 = f32[2,384,1024]{2,1,0:T(8,128)S(1)} custom-call(s32[2]{0:T(128)S(1)} %pad_add_fusion.2.order_ref, bf16[384,4096]{1,0:T(8,128)(2,1)S(1)} %bitcast.55, bf16[4096,8192]{1,0:T(8,128)(2,1)} %bitcast.2.weight_ref), custom_call_target="tpu_custom_call" | custom-call | flops 6442450944 | bytes 19922944 | tf_op jit(solution)/shard_map/chunk_products/pallas_call | solution.py:22
  26.0 0.1 fusion.14
  26.1 0.1 collective-permute-start.6
  26.2 1.3 %pad_add_fusion.1.order_ref = s32[2]{0:T(128)S(1)} fusion(s32[1]{0:T(128)} %get-tuple-element.15, s32[1]{0:T(128)} %get-tuple-element.10), kind=kLoop, calls=%fused_computation.34 | loop fusion | flops 2 | bytes 16 | tf_op jit(solution)/shard_map/concatenate | solution.py:64
  27.4 4.8 %collective-permute-done.2 = f16[384,1024]{1,0:T(8,128)(2,1)S(1)} collective-permute-done((f16[384,1024]{1,0:T(8,128)(2,1)S(1)}, f16[384,1024]{1,0:T(8,128)(2,1)S(1)}, u32[]{:S(2)}, u32[]{:S(2)}) %collective-permute-start.2) | collective-permute-done | bytes 786464 | tf_op jit(solution)/shard_map/ppermute | solution.py:45
  32.2 0.3 fusion.9
  32.5 4.1 %collective-permute-start.3 = (f16[384,1024]{1,0:T(8,128)(2,1)S(1)}, f16[384,1024]{1,0:T(8,128)(2,1)S(1)}, u32[]{:S(2)}, u32[]{:S(2)}) collective-permute-start(f16[384,1024]{1,0:T(8,128)(2,1)S(1)} %fusion.9), channel_id=1, source_target_pairs={{0,4},{2,6},{12,8},{14,10},{1,5},{3,7},{13,9},{15,11},{16,20},{18,... | collective-permute-start | bytes 2359304 | tf_op jit(solution)/shard_map/ppermute | solution.py:45
  36.6 10.7 %chunk_products.5 = f32[2,384,1024]{2,1,0:T(8,128)S(1)} custom-call(s32[2]{0:T(128)S(1)} %pad_add_fusion.1.order_ref, bf16[384,4096]{1,0:T(8,128)(2,1)S(1)} %bitcast.56, bf16[4096,8192]{1,0:T(8,128)(2,1)} %bitcast.2.weight_ref), custom_call_target="tpu_custom_call" | custom-call | flops 6442450944 | bytes 19922944 | tf_op jit(solution)/shard_map/chunk_products/pallas_call | solution.py:22
  47.3 0.1 fusion.13
  47.4 1.6 %collective-permute-start.1 = (f16[384,1024]{1,0:T(8,128)(2,1)S(1)}, f16[384,1024]{1,0:T(8,128)(2,1)S(1)}, u32[]{:S(2)}, u32[]{:S(2)}) collective-permute-start(f16[384,1024]{1,0:T(8,128)(2,1)S(1)} %fusion.13), channel_id=1, source_target_pairs={{0,2},{2,0},{4,6},{6,4},{8,10},{10,8},{12,14},{14,12},{1,3},{3,1},... | collective-permute-start | bytes 2359304 | tf_op jit(solution)/shard_map/ppermute | solution.py:45
  49.0 0.1 slice.46
  49.1 0.7 pad_add_fusion.order_ref
  49.8 0.0 collective-permute-done.6
  49.8 0.3 fusion.10
  50.1 3.4 %collective-permute-start.7 = (f16[384,1024]{1,0:T(8,128)(2,1)S(1)}, f16[384,1024]{1,0:T(8,128)(2,1)S(1)}, u32[]{:S(2)}, u32[]{:S(2)}) collective-permute-start(f16[384,1024]{1,0:T(8,128)(2,1)S(1)} %fusion.10), channel_id=1, source_target_pairs={{0,4},{2,6},{12,8},{14,10},{1,5},{3,7},{13,9},{15,11},{16,20},{18,... | collective-permute-start | bytes 2359304 | tf_op jit(solution)/shard_map/ppermute | solution.py:45
  53.5 0.0 collective-permute-done.3
  53.5 0.4 add_convert_fusion.1
  53.9 0.7 collective-permute-start.4
  54.7 14.9 %chunk_products.4 = f32[3,384,1024]{2,1,0:T(8,128)S(1)} custom-call(s32[3]{0:T(128)S(1)} %pad_add_fusion.order_ref, bf16[384,4096]{1,0:T(8,128)(2,1)S(1)} %bitcast.57, bf16[4096,8192]{1,0:T(8,128)(2,1)} %bitcast.2.weight_ref), custom_call_target="tpu_custom_call" | custom-call | flops 9663676416 | bytes 29884416 | tf_op jit(solution)/shard_map/chunk_products/pallas_call | solution.py:22
  69.5 0.1 fusion.12
  69.7 1.6 %collective-permute-start = (f16[384,1024]{1,0:T(8,128)(2,1)S(1)}, f16[384,1024]{1,0:T(8,128)(2,1)S(1)}, u32[]{:S(2)}, u32[]{:S(2)}) collective-permute-start(f16[384,1024]{1,0:T(8,128)(2,1)S(1)} %fusion.12), channel_id=1, source_target_pairs={{0,2},{2,0},{4,6},{6,4},{8,10},{10,8},{12,14},{14,12},{1,3},{3,1},... | collective-permute-start | bytes 2359304 | tf_op jit(solution)/shard_map/ppermute | solution.py:45
  71.2 0.0 collective-permute-done.7
  71.2 0.5 add_convert_fusion
  71.7 0.0 copy-start.3
  71.7 0.0 copy-start.2
  71.7 0.8 collective-permute-start.8
  72.6 0.0 collective-permute-done.1
  72.6 0.0 collective-permute-done.4
  72.6 0.4 fusion.4
  73.1 4.8 %collective-permute-start.5 = (f16[384,1024]{1,0:T(8,128)(2,1)S(1)}, f16[384,1024]{1,0:T(8,128)(2,1)S(1)}, u32[]{:S(2)}, u32[]{:S(2)}) collective-permute-start(f16[384,1024]{1,0:T(8,128)(2,1)S(1)} %fusion.4), channel_id=1, source_target_pairs={{0,4},{2,6},{4,0},{6,2},{8,12},{10,14},{12,8},{14,10},{1,5},{3,7},... | collective-permute-start | bytes 2359304 | tf_op jit(solution)/shard_map/ppermute | solution.py:45
  77.8 0.0 copy-done.3
  77.8 8.8 %collective-permute-done = f16[384,1024]{1,0:T(8,128)(2,1)S(1)} collective-permute-done((f16[384,1024]{1,0:T(8,128)(2,1)S(1)}, f16[384,1024]{1,0:T(8,128)(2,1)S(1)}, u32[]{:S(2)}, u32[]{:S(2)}) %collective-permute-start) | collective-permute-done | bytes 786464 | tf_op jit(solution)/shard_map/ppermute | solution.py:45
  86.7 0.0 collective-permute-done.8
  86.7 4.9 %collective-permute-done.5 = f16[384,1024]{1,0:T(8,128)(2,1)S(1)} collective-permute-done((f16[384,1024]{1,0:T(8,128)(2,1)S(1)}, f16[384,1024]{1,0:T(8,128)(2,1)S(1)}, u32[]{:S(2)}, u32[]{:S(2)}) %collective-permute-start.5) | collective-permute-done | bytes 786464 | tf_op jit(solution)/shard_map/ppermute | solution.py:45
  91.6 0.0 copy-done.2
  91.6 0.7 multiply_reduce_fusion
  92.3 1.1 %broadcast_multiply_fusion = (f32[384,1024]{1,0:T(8,128)S(1)}, bf16[1,384,1024]{2,1,0:T(8,128)(2,1)}) fusion(f32[384,1024]{1,0:T(8,128)S(1)} %get-tuple-element.3, f32[1024]{0:T(1024)S(1)} %bitcast.58), kind=kLoop, calls=%fused_computation.26 | loop fusion | flops 786432 | bytes 3936256 | tf_op jit(solution)/shard_map/mul | solution.py:124
  93.4 0.0 collective-permute-start.9
  93.4 0.6 collective-permute-start.11
  94.0 0.0 collective-permute-start.10
  94.0 2.4 %collective-permute-done.11 = f32[384]{0:T(512)S(1)} collective-permute-done((f32[384]{0:T(512)S(1)}, f32[384]{0:T(512)S(1)}, u32[]{:S(2)}, u32[]{:S(2)}) %collective-permute-start.11) | collective-permute-done | bytes 1568 | tf_op jit(solution)/shard_map/ppermute | solution.py:102
  96.4 0.4 collective-permute-done.10
  96.8 2.5 %collective-permute-start.14 = (f32[384]{0:T(512)S(1)}, f32[384]{0:T(512)S(1)}, u32[]{:S(2)}, u32[]{:S(2)}) collective-permute-start(f32[384]{0:T(512)S(1)} %add.73), channel_id=1, source_target_pairs={{0,12},{2,14},{4,8},{6,10},{8,4},{10,6},{12,0},{14,2},{1,13},{3,15... | collective-permute-start | bytes 4616 | tf_op jit(solution)/shard_map/ppermute | solution.py:45
  99.3 0.7 collective-permute-start.13
  100.0 1.2 %collective-permute-start.12 = (f32[384]{0:T(512)S(1)}, f32[384]{0:T(512)S(1)}, u32[]{:S(2)}, u32[]{:S(2)}) collective-permute-start(f32[384]{0:T(512)S(1)} %add.73), channel_id=1, source_target_pairs={{0,4},{2,6},{4,0},{6,2},{8,12},{10,14},{12,8},{14,10},{1,5},{3,7},... | collective-permute-start | bytes 4616 | tf_op jit(solution)/shard_map/ppermute | solution.py:45
  101.2 1.0 collective-permute-done.14
  102.2 1.6 %collective-permute-done.13 = f32[384]{0:T(512)S(1)} collective-permute-done((f32[384]{0:T(512)S(1)}, f32[384]{0:T(512)S(1)}, u32[]{:S(2)}, u32[]{:S(2)}) %collective-permute-start.13) | collective-permute-done | bytes 1568 | tf_op jit(solution)/shard_map/ppermute | solution.py:45
  103.8 0.0 collective-permute-done.12
  103.8 0.0 collective-permute-done.9
  103.8 1.0 fusion.11
  (3 shorter events, 0.0 us)
Async XLA Ops:
  2.0 1.9 %copy-start = (bf16[1,384,4096]{2,1,0:T(8,128)(2,1)S(1)}, bf16[1,384,4096]{2,1,0:T(8,128)(2,1)}, u32[]{:S(2)}) copy-start(bf16[1,384,4096]{2,1,0:T(8,128)(2,1)} %param.6) | copy-start | bytes 9437188
  3.9 11.3 %copy-start.1 = (bf16[1,384,4096]{2,1,0:T(8,128)(2,1)S(1)}, bf16[1,384,4096]{2,1,0:T(8,128)(2,1)}, u32[]{:S(2)}) copy-start(bf16[1,384,4096]{2,1,0:T(8,128)(2,1)} %param.6) | copy-start | bytes 9437188
  10.8 21.4 %collective-permute-start.2 = (f16[384,1024]{1,0:T(8,128)(2,1)S(1)}, f16[384,1024]{1,0:T(8,128)(2,1)S(1)}, u32[]{:S(2)}, u32[]{:S(2)}) collective-permute-start(f16[384,1024]{1,0:T(8,128)(2,1)S(1)} %convert_bitcast_fusion.1), channel_id=1, source_target_pairs={{0,2},{2,0},{4,6},{6,4},{8,10},{10,8},{12,14},{14,12},{1,3},{3,1},... | collective-permute-start | bytes 2359304 | tf_op jit(solution)/shard_map/ppermute | solution.py:45
  26.1 23.7 %collective-permute-start.6 = (f16[384,1024]{1,0:T(8,128)(2,1)S(1)}, f16[384,1024]{1,0:T(8,128)(2,1)S(1)}, u32[]{:S(2)}, u32[]{:S(2)}) collective-permute-start(f16[384,1024]{1,0:T(8,128)(2,1)S(1)} %fusion.14), channel_id=1, source_target_pairs={{0,2},{2,0},{4,6},{6,4},{8,10},{10,8},{12,14},{14,12},{1,3},{3,1},... | collective-permute-start | bytes 2359304 | tf_op jit(solution)/shard_map/ppermute | solution.py:45
  32.5 21.0 %collective-permute-start.3 = (f16[384,1024]{1,0:T(8,128)(2,1)S(1)}, f16[384,1024]{1,0:T(8,128)(2,1)S(1)}, u32[]{:S(2)}, u32[]{:S(2)}) collective-permute-start(f16[384,1024]{1,0:T(8,128)(2,1)S(1)} %fusion.9), channel_id=1, source_target_pairs={{0,4},{2,6},{12,8},{14,10},{1,5},{3,7},{13,9},{15,11},{16,20},{18,... | collective-permute-start | bytes 2359304 | tf_op jit(solution)/shard_map/ppermute | solution.py:45
  47.4 25.1 %collective-permute-start.1 = (f16[384,1024]{1,0:T(8,128)(2,1)S(1)}, f16[384,1024]{1,0:T(8,128)(2,1)S(1)}, u32[]{:S(2)}, u32[]{:S(2)}) collective-permute-start(f16[384,1024]{1,0:T(8,128)(2,1)S(1)} %fusion.13), channel_id=1, source_target_pairs={{0,2},{2,0},{4,6},{6,4},{8,10},{10,8},{12,14},{14,12},{1,3},{3,1},... | collective-permute-start | bytes 2359304 | tf_op jit(solution)/shard_map/ppermute | solution.py:45
  50.1 21.1 %collective-permute-start.7 = (f16[384,1024]{1,0:T(8,128)(2,1)S(1)}, f16[384,1024]{1,0:T(8,128)(2,1)S(1)}, u32[]{:S(2)}, u32[]{:S(2)}) collective-permute-start(f16[384,1024]{1,0:T(8,128)(2,1)S(1)} %fusion.10), channel_id=1, source_target_pairs={{0,4},{2,6},{12,8},{14,10},{1,5},{3,7},{13,9},{15,11},{16,20},{18,... | collective-permute-start | bytes 2359304 | tf_op jit(solution)/shard_map/ppermute | solution.py:45
  53.9 18.7 %collective-permute-start.4 = (f16[384,1024]{1,0:T(8,128)(2,1)S(1)}, f16[384,1024]{1,0:T(8,128)(2,1)S(1)}, u32[]{:S(2)}, u32[]{:S(2)}) collective-permute-start(f16[384,1024]{1,0:T(8,128)(2,1)S(1)} %add_convert_fusion.1), channel_id=1, source_target_pairs={{4,8},{6,10},{8,4},{10,6},{5,9},{7,11},{9,5},{11,7},{20,24},{22,26... | collective-permute-start | bytes 2359304 | tf_op jit(solution)/shard_map/ppermute | solution.py:45
  69.7 17.0 %collective-permute-start = (f16[384,1024]{1,0:T(8,128)(2,1)S(1)}, f16[384,1024]{1,0:T(8,128)(2,1)S(1)}, u32[]{:S(2)}, u32[]{:S(2)}) collective-permute-start(f16[384,1024]{1,0:T(8,128)(2,1)S(1)} %fusion.12), channel_id=1, source_target_pairs={{0,2},{2,0},{4,6},{6,4},{8,10},{10,8},{12,14},{14,12},{1,3},{3,1},... | collective-permute-start | bytes 2359304 | tf_op jit(solution)/shard_map/ppermute | solution.py:45
  71.7 6.1 %copy-start.3 = (bf16[1,1024]{1,0:T(2,128)(2,1)S(1)}, bf16[1,1024]{1,0:T(2,128)(2,1)}, u32[]{:S(2)}) copy-start(bf16[1,1024]{1,0:T(2,128)(2,1)} %param.9) | copy-start | bytes 6148
  71.7 19.9 %copy-start.2 = (bf16[1,384,1024]{2,1,0:T(8,128)(2,1)S(1)}, bf16[1,384,1024]{2,1,0:T(8,128)(2,1)}, u32[]{:S(2)}) copy-start(bf16[1,384,1024]{2,1,0:T(8,128)(2,1)} %param.8) | copy-start | bytes 2359300
  71.7 14.9 %collective-permute-start.8 = (f16[384,1024]{1,0:T(8,128)(2,1)S(1)}, f16[384,1024]{1,0:T(8,128)(2,1)S(1)}, u32[]{:S(2)}, u32[]{:S(2)}) collective-permute-start(f16[384,1024]{1,0:T(8,128)(2,1)S(1)} %add_convert_fusion), channel_id=1, source_target_pairs={{4,8},{6,10},{8,4},{10,6},{5,9},{7,11},{9,5},{11,7},{20,24},{22,26... | collective-permute-start | bytes 2359304 | tf_op jit(solution)/shard_map/ppermute | solution.py:45
  73.1 18.5 %collective-permute-start.5 = (f16[384,1024]{1,0:T(8,128)(2,1)S(1)}, f16[384,1024]{1,0:T(8,128)(2,1)S(1)}, u32[]{:S(2)}, u32[]{:S(2)}) collective-permute-start(f16[384,1024]{1,0:T(8,128)(2,1)S(1)} %fusion.4), channel_id=1, source_target_pairs={{0,4},{2,6},{4,0},{6,2},{8,12},{10,14},{12,8},{14,10},{1,5},{3,7},... | collective-permute-start | bytes 2359304 | tf_op jit(solution)/shard_map/ppermute | solution.py:45
  93.4 10.4 %collective-permute-start.9 = (f32[384,1024]{1,0:T(8,128)S(1)}, f32[384,1024]{1,0:T(8,128)S(1)}, u32[]{:S(2)}, u32[]{:S(2)}) collective-permute-start(f32[384,1024]{1,0:T(8,128)S(1)} %get-tuple-element.4), channel_id=1, source_target_pairs={{0,1},{1,0},{2,3},{3,2},{4,5},{5,4},{6,7},{7,6},{8,9},{9,8},{10,11... | collective-permute-start | bytes 4718600 | tf_op jit(solution)/shard_map/ppermute | solution.py:125
  93.4 3.0 %collective-permute-start.11 = (f32[384]{0:T(512)S(1)}, f32[384]{0:T(512)S(1)}, u32[]{:S(2)}, u32[]{:S(2)}) collective-permute-start(f32[384]{0:T(512)S(1)} %get-tuple-element.2), channel_id=1, source_target_pairs={{0,3},{1,2},{2,1},{3,0},{4,7},{5,6},{6,5},{7,4},{8,11},{9,10},{10,... | collective-permute-start | bytes 4616 | tf_op jit(solution)/shard_map/ppermute | solution.py:102
  94.0 2.8 %collective-permute-start.10 = (f32[384]{0:T(512)S(1)}, f32[384]{0:T(512)S(1)}, u32[]{:S(2)}, u32[]{:S(2)}) collective-permute-start(f32[384]{0:T(512)S(1)} %get-tuple-element.2), channel_id=1, source_target_pairs={{0,1},{1,0},{2,3},{3,2},{4,5},{5,4},{6,7},{7,6},{8,9},{9,8},{10,11... | collective-permute-start | bytes 4616 | tf_op jit(solution)/shard_map/ppermute | solution.py:102
  96.8 5.4 %collective-permute-start.14 = (f32[384]{0:T(512)S(1)}, f32[384]{0:T(512)S(1)}, u32[]{:S(2)}, u32[]{:S(2)}) collective-permute-start(f32[384]{0:T(512)S(1)} %add.73), channel_id=1, source_target_pairs={{0,12},{2,14},{4,8},{6,10},{8,4},{10,6},{12,0},{14,2},{1,13},{3,15... | collective-permute-start | bytes 4616 | tf_op jit(solution)/shard_map/ppermute | solution.py:45
  99.3 4.5 %collective-permute-start.13 = (f32[384]{0:T(512)S(1)}, f32[384]{0:T(512)S(1)}, u32[]{:S(2)}, u32[]{:S(2)}) collective-permute-start(f32[384]{0:T(512)S(1)} %add.73), channel_id=1, source_target_pairs={{0,8},{2,10},{4,12},{6,14},{8,0},{10,2},{12,4},{14,6},{1,9},{3,11}... | collective-permute-start | bytes 4616 | tf_op jit(solution)/shard_map/ppermute | solution.py:45
  100.0 3.7 %collective-permute-start.12 = (f32[384]{0:T(512)S(1)}, f32[384]{0:T(512)S(1)}, u32[]{:S(2)}, u32[]{:S(2)}) collective-permute-start(f32[384]{0:T(512)S(1)} %add.73), channel_id=1, source_target_pairs={{0,4},{2,6},{4,0},{6,2},{8,12},{10,14},{12,8},{14,10},{1,5},{3,7},... | collective-permute-start | bytes 4616 | tf_op jit(solution)/shard_map/ppermute | solution.py:45

commit v3 on v2

v3 whole, which is shorter than its diff:
```python
import jax
import jax.numpy as jnp
from jax import lax
from jax.experimental import pallas as pl
from jax.experimental.pallas import tpu as pltpu
from jax.sharding import PartitionSpec as P

F32 = jnp.float32
WIRE = jnp.float16


def tile_products(hidden, weight, place, order, tile):
    rows, depth = hidden.shape
    counts = [len(tiles) for tiles in order]
    starts = [sum(counts[:i]) for i in range(len(counts))]
    listed = [tile for tiles in order for tile in tiles]

    def kernel(place_ref, hidden_ref, weight_ref, *out_refs):
        step = pl.program_id(0)
        for out_ref, start, count in zip(out_refs, starts, counts):

            @pl.when((step >= start) & (step < start + count))
            def _(out_ref=out_ref):
                out_ref[...] = jnp.dot(
                    hidden_ref[...], weight_ref[...], preferred_element_type=F32
                )

    def weight_tile(j, place):
        z, y = place[0] // 2, place[0] % 2
        slots = (3 - 3 * (z // 2), 2 - z // 2, z + 1 - 2 * (z % 2), z)
        places = [4 * slots[s] + 2 * (1 - y if other else y) + half for other, s, half in listed]
        column = places[0]
        for i in range(1, len(places)):
            column = jnp.where(j >= i, places[i], column)
        return (0, column)

    def out_tile(start, count):
        return lambda j, place: (0, jnp.clip(j - start, 0, count - 1))

    return pl.pallas_call(
        kernel,
        out_shape=[jax.ShapeDtypeStruct((rows, n * tile), F32) for n in counts],
        grid_spec=pltpu.PrefetchScalarGridSpec(
            num_scalar_prefetch=1,
            grid=(len(listed),),
            in_specs=[
                pl.BlockSpec((rows, depth), lambda j, place: (0, 0)),
                pl.BlockSpec((depth, tile), weight_tile),
            ],
            out_specs=[
                pl.BlockSpec((rows, tile), out_tile(s, n)) for s, n in zip(starts, counts)
            ],
        ),
        compiler_params=pltpu.CompilerParams(vmem_limit_bytes=32 * 2**20),
        cost_estimate=pl.CostEstimate(
            flops=2 * rows * depth * tile * len(listed),
            bytes_accessed=(2 * depth + 4 * rows) * tile * len(listed),
            transcendentals=0,
        ),
        name="tile_products",
    )(place, hidden, weight)


def send(block, pairs):
    return lax.ppermute(block, "tensor", pairs)


def after(array, *earlier):
    return lax.optimization_barrier((array, *earlier))[0]


def reduce_line_of_four(hidden, weight, width):
    place = lax.axis_index("tensor").astype(jnp.int32)[None]
    tile = width // 2

    across = [(t, t ^ 1) for t in range(8)]
    inward = [(0, 2), (1, 3), (6, 4), (7, 5)]
    middle = [(2, 4), (3, 5), (4, 2), (5, 3)]
    ends = [(t, t ^ 2) for t in range(8)]
    beyond = [(2, 6), (3, 7), (4, 0), (5, 1)]

    def products(order, *earlier):
        here = after(place, *earlier) if earlier else place
        return tile_products(hidden, weight, here, order, tile)

    def theirs(slot, *halves):
        return [(1, slot, half) for half in halves or (0, 1)]

    def mine(slot, *halves):
        return [(0, slot, half) for half in halves or (0, 1)]

    def narrow(block):
        return block.astype(WIRE)

    def wide(block):
        return block.astype(F32)

    def join(left, right):
        return jnp.concatenate([left, right], axis=1)

    [first] = products([theirs(0, 0)])
    first = narrow(first)
    y0a = send(first, across)
    second, own0a = products([theirs(0, 1), mine(0, 0)], first)
    second = narrow(second)
    y0b = send(second, across)
    third, own0b = products([theirs(1), mine(0, 1)], second, y0a)
    third = narrow(third)
    y1 = send(third, across)
    sum0 = join(own0a + wide(y0a), own0b + wide(after(y0b, third)))
    out0 = narrow(sum0)
    in0 = send(out0, inward)
    fourth, own1 = products([theirs(2), mine(1)], third, out0)
    fourth = narrow(fourth)
    y2 = send(fourth, across)
    sum1 = own1 + wide(after(y1, own1))
    out1 = narrow(sum1)
    in1 = send(out1, inward)
    passed0 = narrow(sum0 + wide(after(in0, out1)))
    far0 = send(passed0, beyond)
    fifth, own2 = products([theirs(3), mine(2)], fourth, out1, passed0)
    fifth = narrow(fifth)
    y3 = send(fifth, across)
    passed1 = narrow(sum1 + wide(after(in1, own2)))
    mid1 = send(passed1, middle)
    out2 = narrow(own2 + wide(after(y2, own2)))
    last = send(out2, ends)
    [own3] = products([mine(3)], fifth, out2, passed1)
    return own3 + wide(y3) + wide(last) + wide(far0) + wide(mid1)


def total_squares(squares, count):
    swap = [(0, 1), (1, 0)]
    if count != 8:
        squares = lax.ppermute(squares, "section", swap)
        step = 1
        while step < count:
            squares = squares + send(squares, [(t, t ^ step) for t in range(count)])
            step *= 2
        return squares
    corner = [(2 * t + s, 2 * (t ^ 1) + 1 - s) for t in range(8) for s in range(2)]
    squares = lax.ppermute(squares, "section", swap) + lax.ppermute(
        squares, ("tensor", "section"), corner
    )
    others = [send(squares, [(t, t ^ step) for t in range(8)]) for step in (2, 4, 6)]
    return squares + others[0] + (others[1] + others[2])


def per_device(hidden, down_weight, stream, norm_gain):
    count = lax.axis_size("tensor")
    full_width = down_weight.shape[2]
    width = full_width // count
    if count == 8:
        projected = reduce_line_of_four(hidden[0], down_weight[0], width)
    else:
        projected = lax.psum_scatter(
            jnp.dot(hidden[0], down_weight[0], preferred_element_type=F32),
            "tensor",
            scatter_dimension=1,
            tiled=True,
        )
    updated = stream[0].astype(F32) + projected
    squares = total_squares(jnp.sum(updated * updated, axis=1), count)
    scaled = updated * norm_gain[0].astype(F32)[None, :]
    passed = lax.ppermute(scaled, "section", [(0, 1), (1, 0)])
    inverse = lax.rsqrt(squares / full_width + 1e-05)
    normed = (passed * inverse[:, None]).astype(jnp.bfloat16)
    return (updated.astype(jnp.bfloat16)[None], normed[None])


def solution(mesh):
    in_specs = (
        P("section", "groups", "tensor"),
        P("section", "tensor", None),
        P("section", "groups", "tensor"),
        P("section", "tensor"),
    )
    out_specs = (P("section", "groups", "tensor"), P("section", "groups", "tensor"))
    return jax.shard_map(
        per_device, mesh=mesh, in_specs=in_specs, out_specs=out_specs, check_vma=False
    )
```

time: 105 us -> 99.7 us (0.950)
  waiting for transfers between devices: 24 us -> 19.5 us
  other arithmetic: 9.19 us -> 4.97 us
  Pallas kernels: 43.1 us -> 45 us
  starting transfers between devices: 25.1 us -> 27 us
    ppermute x12 -> x13, waiting for transfers between devices: 21.1 us -> 17.5 us  [send(): return lax.ppermute(block, 'tensor', pairs)]
    concatenate x3 -> x0, other arithmetic: 3.3 us -> none  [both(): return chunk_products(hidden, weight, jnp.concatenate(indices), width)]
    ppermute x1, waiting for transfers between devices: 2.4 us -> 0.11 us  [total_squares(): lax.ppermute(squares, ('tensor', 'section'), corner)]
    pallas_call x4 -> x6, Pallas kernels: 43.1 us -> 45 us  [tile_products(): pl.pallas_call(kernel, out_shape=[jax.ShapeDtypeStruct((rows, n * tile),...]
    ppermute x1, waiting for transfers between devices: 0.4 us -> 1.87 us  [total_squares(): lax.ppermute(squares, 'section', swap)]
    ppermute x12 -> x13, starting transfers between devices: 24.4 us -> 25.4 us  [send(): return lax.ppermute(block, 'tensor', pairs)]
    convert_element_type x9 -> x10, other arithmetic: 2.36 us -> 1.77 us  [narrow(): return block.astype(WIRE)]
  transfers between devices with their start and end apart: 15 -> 16, of which waited for: 7 -> 7; matrix products, arithmetic and copies ran while one was open for 5% -> 2% of each run, Pallas kernels for 35% -> 41%
where the time goes in v3:
time: 99.7 us; the launch traced here: 99.2 us
  Pallas kernels  45 us (45%)
  starting transfers between devices  27 us (27%)
  waiting for transfers between devices  19.5 us (20%)
  other arithmetic  4.97 us (5%)
  local copies, waits for them, and re-layouts  1.9 us (2%)
    pallas_call x6, Pallas kernels, tile_products(): pl.pallas_call(kernel, out_shape=[jax.ShapeDtypeStruct((rows, n * tile),...  45 us
    ppermute x13, starting transfers between devices, send(): return lax.ppermute(block, 'tensor', pairs)  25.4 us
    ppermute x13, waiting for transfers between devices, send(): return lax.ppermute(block, 'tensor', pairs)  17.5 us
  transfers between devices with their start and end apart: 16, of which 7 were waited for; matrix products, arithmetic and copies ran while one was open for 2% of the time, Pallas kernels for 41%

profile of v3, /device:TPU:0, one launch (start us, length us, event | category | flops | bytes accessed | tf_op | source)
XLA Modules:
  0.0 99.2 jit_solution(17605265821412498431)
XLA Ops:
  0.6 0.0 copy-start
  0.6 1.9 %copy-done = bf16[1,384,4096]{2,1,0:T(8,128)(2,1)S(1)} copy-done((bf16[1,384,4096]{2,1,0:T(8,128)(2,1)S(1)}, bf16[1,384,4096]{2,1,0:T(8,128)(2,1)}, u32[]{:S(2)}) %copy-start) | copy-done | bytes 3145752
  2.5 4.0 %tile_products.6 = f32[384,512]{1,0:T(8,128)S(1)} custom-call(s32[1]{0:T(128)} %bitcast.1.place_ref, bf16[384,4096]{1,0:T(8,128)(2,1)S(1)} %bitcast.12, bf16[4096,8192]{1,0:T(8,128)(2,1)} %bitcast.3.weight_ref), custom_call_target="tpu_custom_call" | custom-call | flops 1610612736 | bytes 4980736 | tf_op jit(solution)/shard_map/tile_products/pallas_call | solution.py:40
  6.6 0.1 convert_element_type.76
  6.6 3.0 %collective-permute-start = (f16[384,512]{1,0:T(8,128)(2,1)S(1)}, f16[384,512]{1,0:T(8,128)(2,1)S(1)}, u32[]{:S(2)}, u32[]{:S(2)}) collective-permute-start(f16[384,512]{1,0:T(8,128)(2,1)S(1)} %convert_element_type.76), channel_id=1, source_target_pairs={{0,2},{2,0},{4,6},{6,4},{8,10},{10,8},{12,14},{14,12},{1,3},{3,1},... | collective-permute-start | bytes 1179656 | tf_op jit(solution)/shard_map/ppermute | solution.py:65
  9.7 5.9 %tile_products.7 = (f32[384,512]{1,0:T(8,128)S(1)}, f32[384,512]{1,0:T(8,128)S(1)}) custom-call(s32[1]{0:T(128)} %bitcast.1.place_ref, bf16[384,4096]{1,0:T(8,128)(2,1)S(1)} %bitcast.13, bf16[4096,8192]{1,0:T(8,128)(2,1)} %bitcast.3.weight_ref), custom_call_target="tpu_custom_call" | custom-call | flops 3221225472 | bytes 9961472 | tf_op jit(solution)/shard_map/tile_products/pallas_call | solution.py:40
  15.6 0.1 convert_element_type.77
  15.7 0.1 collective-permute-start.1
  15.8 3.8 %collective-permute-done = f16[384,512]{1,0:T(8,128)(2,1)S(1)} collective-permute-done((f16[384,512]{1,0:T(8,128)(2,1)S(1)}, f16[384,512]{1,0:T(8,128)(2,1)S(1)}, u32[]{:S(2)}, u32[]{:S(2)}) %collective-permute-start) | collective-permute-done | bytes 393248 | tf_op jit(solution)/shard_map/ppermute | solution.py:65
  19.6 8.2 %tile_products.8 = (f32[384,1024]{1,0:T(8,128)S(1)}, f32[384,512]{1,0:T(8,128)S(1)}) custom-call(s32[1]{0:T(128)} %bitcast.1.place_ref, bf16[384,4096]{1,0:T(8,128)(2,1)S(1)} %bitcast.14, bf16[4096,8192]{1,0:T(8,128)(2,1)} %bitcast.3.weight_ref), custom_call_target="tpu_custom_call" | custom-call | flops 4831838208 | bytes 14942208 | tf_op jit(solution)/shard_map/tile_products/pallas_call | solution.py:40
  27.9 0.1 convert_element_type.78
  28.0 2.1 %collective-permute-start.2 = (f16[384,1024]{1,0:T(8,128)(2,1)S(1)}, f16[384,1024]{1,0:T(8,128)(2,1)S(1)}, u32[]{:S(2)}, u32[]{:S(2)}) collective-permute-start(f16[384,1024]{1,0:T(8,128)(2,1)S(1)} %convert_element_type.78), channel_id=1, source_target_pairs={{0,2},{2,0},{4,6},{6,4},{8,10},{10,8},{12,14},{14,12},{1,3},{3,1},... | collective-permute-start | bytes 2359304 | tf_op jit(solution)/shard_map/ppermute | solution.py:65
  30.1 0.0 collective-permute-done.1
  30.1 0.1 convert_add_fusion.2
  30.2 0.1 convert_add_fusion.3
  30.4 0.1 fusion
  30.5 3.5 %collective-permute-start.3 = (f16[384,1024]{1,0:T(8,128)(2,1)S(1)}, f16[384,1024]{1,0:T(8,128)(2,1)S(1)}, u32[]{:S(2)}, u32[]{:S(2)}) collective-permute-start(f16[384,1024]{1,0:T(8,128)(2,1)S(1)} %fusion), channel_id=1, source_target_pairs={{0,4},{2,6},{12,8},{14,10},{1,5},{3,7},{13,9},{15,11},{16,20},{18,... | collective-permute-start | bytes 2359304 | tf_op jit(solution)/shard_map/ppermute | solution.py:65
  34.0 10.3 %tile_products.9 = (f32[384,1024]{1,0:T(8,128)S(1)}, f32[384,1024]{1,0:T(8,128)S(1)}) custom-call(s32[1]{0:T(128)} %bitcast.1.place_ref, bf16[384,4096]{1,0:T(8,128)(2,1)S(1)} %bitcast.15, bf16[4096,8192]{1,0:T(8,128)(2,1)} %bitcast.3.weight_ref), custom_call_target="tpu_custom_call" | custom-call | flops 6442450944 | bytes 19922944 | tf_op jit(solution)/shard_map/tile_products/pallas_call | solution.py:40
  44.4 0.1 convert_element_type.82
  44.5 0.5 collective-permute-start.4
  44.9 2.5 %collective-permute-done.2 = f16[384,1024]{1,0:T(8,128)(2,1)S(1)} collective-permute-done((f16[384,1024]{1,0:T(8,128)(2,1)S(1)}, f16[384,1024]{1,0:T(8,128)(2,1)S(1)}, u32[]{:S(2)}, u32[]{:S(2)}) %collective-permute-start.2) | collective-permute-done | bytes 786464 | tf_op jit(solution)/shard_map/ppermute | solution.py:65
  47.4 0.3 fusion.1
  47.7 5.1 %collective-permute-start.5 = (f16[384,1024]{1,0:T(8,128)(2,1)S(1)}, f16[384,1024]{1,0:T(8,128)(2,1)S(1)}, u32[]{:S(2)}, u32[]{:S(2)}) collective-permute-start(f16[384,1024]{1,0:T(8,128)(2,1)S(1)} %fusion.1), channel_id=1, source_target_pairs={{0,4},{2,6},{12,8},{14,10},{1,5},{3,7},{13,9},{15,11},{16,20},{18,... | collective-permute-start | bytes 2359304 | tf_op jit(solution)/shard_map/ppermute | solution.py:65
  52.8 0.0 collective-permute-done.3
  52.8 0.3 add_convert_fusion.2
  53.0 1.3 %collective-permute-start.8 = (f16[384,1024]{1,0:T(8,128)(2,1)S(1)}, f16[384,1024]{1,0:T(8,128)(2,1)S(1)}, u32[]{:S(2)}, u32[]{:S(2)}) collective-permute-start(f16[384,1024]{1,0:T(8,128)(2,1)S(1)} %add_convert_fusion.2), channel_id=1, source_target_pairs={{4,12},{6,14},{8,0},{10,2},{5,13},{7,15},{9,1},{11,3},{20,28},{22,... | collective-permute-start | bytes 2359304 | tf_op jit(solution)/shard_map/ppermute | solution.py:65
  54.3 10.3 %tile_products.10 = (f32[384,1024]{1,0:T(8,128)S(1)}, f32[384,1024]{1,0:T(8,128)S(1)}) custom-call(s32[1]{0:T(128)} %bitcast.1.place_ref, bf16[384,4096]{1,0:T(8,128)(2,1)S(1)} %bitcast.16, bf16[4096,8192]{1,0:T(8,128)(2,1)} %bitcast.3.weight_ref), custom_call_target="tpu_custom_call" | custom-call | flops 6442450944 | bytes 19922944 | tf_op jit(solution)/shard_map/tile_products/pallas_call | solution.py:40
  64.7 0.0 collective-permute-done.4
  64.7 0.3 add_convert_fusion.1
  65.0 3.8 %collective-permute-start.7 = (f16[384,1024]{1,0:T(8,128)(2,1)S(1)}, f16[384,1024]{1,0:T(8,128)(2,1)S(1)}, u32[]{:S(2)}, u32[]{:S(2)}) collective-permute-start(f16[384,1024]{1,0:T(8,128)(2,1)S(1)} %add_convert_fusion.1), channel_id=1, source_target_pairs={{0,4},{2,6},{4,0},{6,2},{8,12},{10,14},{12,8},{14,10},{1,5},{3,7},... | collective-permute-start | bytes 2359304 | tf_op jit(solution)/shard_map/ppermute | solution.py:65
  68.7 0.1 convert_element_type.87
  68.8 0.0 copy-start.2
  68.9 1.7 %collective-permute-start.6 = (f16[384,1024]{1,0:T(8,128)(2,1)S(1)}, f16[384,1024]{1,0:T(8,128)(2,1)S(1)}, u32[]{:S(2)}, u32[]{:S(2)}) collective-permute-start(f16[384,1024]{1,0:T(8,128)(2,1)S(1)} %convert_element_type.87), channel_id=1, source_target_pairs={{0,2},{2,0},{4,6},{6,4},{8,10},{10,8},{12,14},{14,12},{1,3},{3,1},... | collective-permute-start | bytes 2359304 | tf_op jit(solution)/shard_map/ppermute | solution.py:65
  70.5 0.0 collective-permute-done.5
  70.5 0.4 add_convert_fusion
  71.0 0.9 collective-permute-start.9
  71.9 0.0 copy-done.2
  71.9 0.0 copy-start.1
  71.9 6.1 %tile_products.11 = f32[384,1024]{1,0:T(8,128)S(1)} custom-call(s32[1]{0:T(128)} %bitcast.1.place_ref, bf16[384,4096]{1,0:T(8,128)(2,1)S(1)} %bitcast.17, bf16[4096,8192]{1,0:T(8,128)(2,1)} %bitcast.3.weight_ref), custom_call_target="tpu_custom_call" | custom-call | flops 3221225472 | bytes 9961472 | tf_op jit(solution)/shard_map/tile_products/pallas_call | solution.py:40
  78.1 0.0 collective-permute-done.8
  78.1 7.6 %collective-permute-done.7 = f16[384,1024]{1,0:T(8,128)(2,1)S(1)} collective-permute-done((f16[384,1024]{1,0:T(8,128)(2,1)S(1)}, f16[384,1024]{1,0:T(8,128)(2,1)S(1)}, u32[]{:S(2)}, u32[]{:S(2)}) %collective-permute-start.7) | collective-permute-done | bytes 786464 | tf_op jit(solution)/shard_map/ppermute | solution.py:65
  85.7 0.0 collective-permute-done.6
  85.7 0.0 collective-permute-done.9
  85.7 0.0 copy-done.1
  85.7 0.8 multiply_reduce_fusion
  86.5 1.1 %broadcast_multiply_fusion = (f32[384,1024]{1,0:T(8,128)S(1)}, bf16[1,384,1024]{2,1,0:T(8,128)(2,1)}) fusion(f32[384,1024]{1,0:T(8,128)S(1)} %get-tuple-element.39, f32[1024]{0:T(1024)S(1)} %bitcast.18), kind=kLoop, calls=%fused_computation.11 | loop fusion | flops 786432 | bytes 3936256 | tf_op jit(solution)/shard_map/mul | solution.py:164
  87.7 0.0 collective-permute-start.10
  87.7 0.5 collective-permute-start.11
  88.2 1.0 %collective-permute-start.12 = (f32[384]{0:T(512)S(1)}, f32[384]{0:T(512)S(1)}, u32[]{:S(2)}, u32[]{:S(2)}) collective-permute-start(f32[384]{0:T(512)S(1)} %get-tuple-element.38), channel_id=1, source_target_pairs={{0,3},{1,2},{2,1},{3,0},{4,7},{5,6},{6,5},{7,4},{8,11},{9,10},{10,... | collective-permute-start | bytes 4616 | tf_op jit(solution)/shard_map/ppermute | solution.py:142
  89.2 1.9 %collective-permute-done.11 = f32[384]{0:T(512)S(1)} collective-permute-done((f32[384]{0:T(512)S(1)}, f32[384]{0:T(512)S(1)}, u32[]{:S(2)}, u32[]{:S(2)}) %collective-permute-start.11) | collective-permute-done | bytes 1568 | tf_op jit(solution)/shard_map/ppermute | solution.py:142
  91.1 0.1 collective-permute-done.12
  91.2 1.6 %collective-permute-start.14 = (f32[384]{0:T(512)S(1)}, f32[384]{0:T(512)S(1)}, u32[]{:S(2)}, u32[]{:S(2)}) collective-permute-start(f32[384]{0:T(512)S(1)} %add.62), channel_id=1, source_target_pairs={{0,8},{2,10},{4,12},{6,14},{8,0},{10,2},{12,4},{14,6},{1,9},{3,11}... | collective-permute-start | bytes 4616 | tf_op jit(solution)/shard_map/ppermute | solution.py:65
  92.8 1.3 %collective-permute-start.15 = (f32[384]{0:T(512)S(1)}, f32[384]{0:T(512)S(1)}, u32[]{:S(2)}, u32[]{:S(2)}) collective-permute-start(f32[384]{0:T(512)S(1)} %add.62), channel_id=1, source_target_pairs={{0,12},{2,14},{4,8},{6,10},{8,4},{10,6},{12,0},{14,2},{1,13},{3,15... | collective-permute-start | bytes 4616 | tf_op jit(solution)/shard_map/ppermute | solution.py:65
  94.1 0.5 collective-permute-start.13
  94.7 1.0 %collective-permute-done.14 = f32[384]{0:T(512)S(1)} collective-permute-done((f32[384]{0:T(512)S(1)}, f32[384]{0:T(512)S(1)}, u32[]{:S(2)}, u32[]{:S(2)}) %collective-permute-start.14) | collective-permute-done | bytes 1568 | tf_op jit(solution)/shard_map/ppermute | solution.py:65
  95.7 2.5 %collective-permute-done.15 = f32[384]{0:T(512)S(1)} collective-permute-done((f32[384]{0:T(512)S(1)}, f32[384]{0:T(512)S(1)}, u32[]{:S(2)}, u32[]{:S(2)}) %collective-permute-start.15) | collective-permute-done | bytes 1568 | tf_op jit(solution)/shard_map/ppermute | solution.py:65
  98.2 0.0 collective-permute-done.13
  98.2 0.0 collective-permute-done.10
  98.2 1.0 %fusion.2 = bf16[1,384,1024]{2,1,0:T(8,128)(2,1)} fusion(f32[384,1024]{1,0:T(8,128)S(1)} %collective-permute-done.10, f32[384]{0:T(512)S(1)} %add_rsqrt_fusion), kind=kLoop, calls=%fused_computation.10 | loop fusion | flops 786432 | bytes 2360832 | tf_op jit(solution)/shard_map/broadcast_in_dim | solution.py:168
  (3 shorter events, 0.0 us)
Async XLA Ops:
  0.6 1.9 %copy-start = (bf16[1,384,4096]{2,1,0:T(8,128)(2,1)S(1)}, bf16[1,384,4096]{2,1,0:T(8,128)(2,1)}, u32[]{:S(2)}) copy-start(bf16[1,384,4096]{2,1,0:T(8,128)(2,1)} %param.4) | copy-start | bytes 9437188
  6.6 13.0 %collective-permute-start = (f16[384,512]{1,0:T(8,128)(2,1)S(1)}, f16[384,512]{1,0:T(8,128)(2,1)S(1)}, u32[]{:S(2)}, u32[]{:S(2)}) collective-permute-start(f16[384,512]{1,0:T(8,128)(2,1)S(1)} %convert_element_type.76), channel_id=1, source_target_pairs={{0,2},{2,0},{4,6},{6,4},{8,10},{10,8},{12,14},{14,12},{1,3},{3,1},... | collective-permute-start | bytes 1179656 | tf_op jit(solution)/shard_map/ppermute | solution.py:65
  15.7 14.4 %collective-permute-start.1 = (f16[384,512]{1,0:T(8,128)(2,1)S(1)}, f16[384,512]{1,0:T(8,128)(2,1)S(1)}, u32[]{:S(2)}, u32[]{:S(2)}) collective-permute-start(f16[384,512]{1,0:T(8,128)(2,1)S(1)} %convert_element_type.77), channel_id=1, source_target_pairs={{0,2},{2,0},{4,6},{6,4},{8,10},{10,8},{12,14},{14,12},{1,3},{3,1},... | collective-permute-start | bytes 1179656 | tf_op jit(solution)/shard_map/ppermute | solution.py:65
  28.0 19.5 %collective-permute-start.2 = (f16[384,1024]{1,0:T(8,128)(2,1)S(1)}, f16[384,1024]{1,0:T(8,128)(2,1)S(1)}, u32[]{:S(2)}, u32[]{:S(2)}) collective-permute-start(f16[384,1024]{1,0:T(8,128)(2,1)S(1)} %convert_element_type.78), channel_id=1, source_target_pairs={{0,2},{2,0},{4,6},{6,4},{8,10},{10,8},{12,14},{14,12},{1,3},{3,1},... | collective-permute-start | bytes 2359304 | tf_op jit(solution)/shard_map/ppermute | solution.py:65
  30.5 22.3 %collective-permute-start.3 = (f16[384,1024]{1,0:T(8,128)(2,1)S(1)}, f16[384,1024]{1,0:T(8,128)(2,1)S(1)}, u32[]{:S(2)}, u32[]{:S(2)}) collective-permute-start(f16[384,1024]{1,0:T(8,128)(2,1)S(1)} %fusion), channel_id=1, source_target_pairs={{0,4},{2,6},{12,8},{14,10},{1,5},{3,7},{13,9},{15,11},{16,20},{18,... | collective-permute-start | bytes 2359304 | tf_op jit(solution)/shard_map/ppermute | solution.py:65
  44.5 20.2 %collective-permute-start.4 = (f16[384,1024]{1,0:T(8,128)(2,1)S(1)}, f16[384,1024]{1,0:T(8,128)(2,1)S(1)}, u32[]{:S(2)}, u32[]{:S(2)}) collective-permute-start(f16[384,1024]{1,0:T(8,128)(2,1)S(1)} %convert_element_type.82), channel_id=1, source_target_pairs={{0,2},{2,0},{4,6},{6,4},{8,10},{10,8},{12,14},{14,12},{1,3},{3,1},... | collective-permute-start | bytes 2359304 | tf_op jit(solution)/shard_map/ppermute | solution.py:65
  47.7 22.8 %collective-permute-start.5 = (f16[384,1024]{1,0:T(8,128)(2,1)S(1)}, f16[384,1024]{1,0:T(8,128)(2,1)S(1)}, u32[]{:S(2)}, u32[]{:S(2)}) collective-permute-start(f16[384,1024]{1,0:T(8,128)(2,1)S(1)} %fusion.1), channel_id=1, source_target_pairs={{0,4},{2,6},{12,8},{14,10},{1,5},{3,7},{13,9},{15,11},{16,20},{18,... | collective-permute-start | bytes 2359304 | tf_op jit(solution)/shard_map/ppermute | solution.py:65
  53.0 25.0 %collective-permute-start.8 = (f16[384,1024]{1,0:T(8,128)(2,1)S(1)}, f16[384,1024]{1,0:T(8,128)(2,1)S(1)}, u32[]{:S(2)}, u32[]{:S(2)}) collective-permute-start(f16[384,1024]{1,0:T(8,128)(2,1)S(1)} %add_convert_fusion.2), channel_id=1, source_target_pairs={{4,12},{6,14},{8,0},{10,2},{5,13},{7,15},{9,1},{11,3},{20,28},{22,... | collective-permute-start | bytes 2359304 | tf_op jit(solution)/shard_map/ppermute | solution.py:65
  65.0 20.8 %collective-permute-start.7 = (f16[384,1024]{1,0:T(8,128)(2,1)S(1)}, f16[384,1024]{1,0:T(8,128)(2,1)S(1)}, u32[]{:S(2)}, u32[]{:S(2)}) collective-permute-start(f16[384,1024]{1,0:T(8,128)(2,1)S(1)} %add_convert_fusion.1), channel_id=1, source_target_pairs={{0,4},{2,6},{4,0},{6,2},{8,12},{10,14},{12,8},{14,10},{1,5},{3,7},... | collective-permute-start | bytes 2359304 | tf_op jit(solution)/shard_map/ppermute | solution.py:65
  68.8 3.0 %copy-start.2 = (bf16[1,1024]{1,0:T(2,128)(2,1)S(1)}, bf16[1,1024]{1,0:T(2,128)(2,1)}, u32[]{:S(2)}) copy-start(bf16[1,1024]{1,0:T(2,128)(2,1)} %param.7) | copy-start | bytes 6148
  68.9 16.9 %collective-permute-start.6 = (f16[384,1024]{1,0:T(8,128)(2,1)S(1)}, f16[384,1024]{1,0:T(8,128)(2,1)S(1)}, u32[]{:S(2)}, u32[]{:S(2)}) collective-permute-start(f16[384,1024]{1,0:T(8,128)(2,1)S(1)} %convert_element_type.87), channel_id=1, source_target_pairs={{0,2},{2,0},{4,6},{6,4},{8,10},{10,8},{12,14},{14,12},{1,3},{3,1},... | collective-permute-start | bytes 2359304 | tf_op jit(solution)/shard_map/ppermute | solution.py:65
  71.0 14.8 %collective-permute-start.9 = (f16[384,1024]{1,0:T(8,128)(2,1)S(1)}, f16[384,1024]{1,0:T(8,128)(2,1)S(1)}, u32[]{:S(2)}, u32[]{:S(2)}) collective-permute-start(f16[384,1024]{1,0:T(8,128)(2,1)S(1)} %add_convert_fusion), channel_id=1, source_target_pairs={{4,8},{6,10},{8,4},{10,6},{5,9},{7,11},{9,5},{11,7},{20,24},{22,26... | collective-permute-start | bytes 2359304 | tf_op jit(solution)/shard_map/ppermute | solution.py:65
  71.9 13.8 %copy-start.1 = (bf16[1,384,1024]{2,1,0:T(8,128)(2,1)S(1)}, bf16[1,384,1024]{2,1,0:T(8,128)(2,1)}, u32[]{:S(2)}) copy-start(bf16[1,384,1024]{2,1,0:T(8,128)(2,1)} %param.6) | copy-start | bytes 2359300
  87.7 10.5 %collective-permute-start.10 = (f32[384,1024]{1,0:T(8,128)S(1)}, f32[384,1024]{1,0:T(8,128)S(1)}, u32[]{:S(2)}, u32[]{:S(2)}) collective-permute-start(f32[384,1024]{1,0:T(8,128)S(1)} %get-tuple-element.40), channel_id=1, source_target_pairs={{0,1},{1,0},{2,3},{3,2},{4,5},{5,4},{6,7},{7,6},{8,9},{9,8},{10,11... | collective-permute-start | bytes 4718600 | tf_op jit(solution)/shard_map/ppermute | solution.py:165
  87.7 3.4 %collective-permute-start.11 = (f32[384]{0:T(512)S(1)}, f32[384]{0:T(512)S(1)}, u32[]{:S(2)}, u32[]{:S(2)}) collective-permute-start(f32[384]{0:T(512)S(1)} %get-tuple-element.38), channel_id=1, source_target_pairs={{0,1},{1,0},{2,3},{3,2},{4,5},{5,4},{6,7},{7,6},{8,9},{9,8},{10,11... | collective-permute-start | bytes 4616 | tf_op jit(solution)/shard_map/ppermute | solution.py:142
  88.2 3.0 %collective-permute-start.12 = (f32[384]{0:T(512)S(1)}, f32[384]{0:T(512)S(1)}, u32[]{:S(2)}, u32[]{:S(2)}) collective-permute-start(f32[384]{0:T(512)S(1)} %get-tuple-element.38), channel_id=1, source_target_pairs={{0,3},{1,2},{2,1},{3,0},{4,7},{5,6},{6,5},{7,4},{8,11},{9,10},{10,... | collective-permute-start | bytes 4616 | tf_op jit(solution)/shard_map/ppermute | solution.py:142
  91.2 4.5 %collective-permute-start.14 = (f32[384]{0:T(512)S(1)}, f32[384]{0:T(512)S(1)}, u32[]{:S(2)}, u32[]{:S(2)}) collective-permute-start(f32[384]{0:T(512)S(1)} %add.62), channel_id=1, source_target_pairs={{0,8},{2,10},{4,12},{6,14},{8,0},{10,2},{12,4},{14,6},{1,9},{3,11}... | collective-permute-start | bytes 4616 | tf_op jit(solution)/shard_map/ppermute | solution.py:65
  92.8 5.4 %collective-permute-start.15 = (f32[384]{0:T(512)S(1)}, f32[384]{0:T(512)S(1)}, u32[]{:S(2)}, u32[]{:S(2)}) collective-permute-start(f32[384]{0:T(512)S(1)} %add.62), channel_id=1, source_target_pairs={{0,12},{2,14},{4,8},{6,10},{8,4},{10,6},{12,0},{14,2},{1,13},{3,15... | collective-permute-start | bytes 4616 | tf_op jit(solution)/shard_map/ppermute | solution.py:65
  94.1 4.0 %collective-permute-start.13 = (f32[384]{0:T(512)S(1)}, f32[384]{0:T(512)S(1)}, u32[]{:S(2)}, u32[]{:S(2)}) collective-permute-start(f32[384]{0:T(512)S(1)} %add.62), channel_id=1, source_target_pairs={{0,4},{2,6},{4,0},{6,2},{8,12},{10,14},{12,8},{14,10},{1,5},{3,7},... | collective-permute-start | bytes 4616 | tf_op jit(solution)/shard_map/ppermute | solution.py:65

commit v4 on v3

--- a/solution.py
+++ b/solution.py
@@ -98,7 +98,13 @@
     def join(left, right):
         return jnp.concatenate([left, right], axis=1)
 
-    [first] = products([theirs(0, 0)])
+    me = lax.axis_index("tensor")
+    column = 4 * (3 - 3 * (me // 4)) + 2 * (1 - me % 2)
+    first = jnp.dot(
+        hidden,
+        lax.dynamic_slice_in_dim(weight, column * tile, tile, 1),
+        preferred_element_type=F32,
+    )
     first = narrow(first)
     y0a = send(first, across)
     second, own0a = products([theirs(0, 1), mine(0, 0)], first)
@@ -107,7 +113,7 @@
     third, own0b = products([theirs(1), mine(0, 1)], second, y0a)
     third = narrow(third)
     y1 = send(third, across)
-    sum0 = join(own0a + wide(y0a), own0b + wide(after(y0b, third)))
+    sum0 = join(own0a, own0b) + wide(join(y0a, after(y0b, own0b)))
     out0 = narrow(sum0)
     in0 = send(out0, inward)
     fourth, own1 = products([theirs(2), mine(1)], third, out0)
@@ -121,29 +127,34 @@
     fifth, own2 = products([theirs(3), mine(2)], fourth, out1, passed0)
     fifth = narrow(fifth)
     y3 = send(fifth, across)
-    passed1 = narrow(sum1 + wide(after(in1, own2)))
+    passed1 = narrow(sum1 + wide(after(in1, fifth)))
     mid1 = send(passed1, middle)
-    out2 = narrow(own2 + wide(after(y2, own2)))
+    out2 = narrow(own2 + wide(after(y2, passed1)))
     last = send(out2, ends)
     [own3] = products([mine(3)], fifth, out2, passed1)
     return own3 + wide(y3) + wide(last) + wide(far0) + wide(mid1)
 
 
-def total_squares(squares, count):
-    swap = [(0, 1), (1, 0)]
-    if count != 8:
-        squares = lax.ppermute(squares, "section", swap)
-        step = 1
-        while step < count:
-            squares = squares + send(squares, [(t, t ^ step) for t in range(count)])
-            step *= 2
-        return squares
-    corner = [(2 * t + s, 2 * (t ^ 1) + 1 - s) for t in range(8) for s in range(2)]
-    squares = lax.ppermute(squares, "section", swap) + lax.ppermute(
-        squares, ("tensor", "section"), corner
-    )
-    others = [send(squares, [(t, t ^ step) for t in range(8)]) for step in (2, 4, 6)]
-    return squares + others[0] + (others[1] + others[2])
+def swapped(block):
+    return lax.ppermute(block, "section", [(0, 1), (1, 0)])
+
+
+def first_round(squares, count):
+    if count == 1:
+        return swapped(squares)
+    corner = [(2 * t + s, 2 * (t ^ 1) + 1 - s) for t in range(count) for s in range(2)]
+    return swapped(squares) + lax.ppermute(squares, ("tensor", "section"), corner)
+
+
+def other_rounds(squares, count):
+    if count == 8:
+        near, far, beyond = [send(squares, [(t, t ^ step) for t in range(8)]) for step in (2, 4, 6)]
+        return squares + near + (far + beyond)
+    step = 2
+    while step < count:
+        squares = squares + send(squares, [(t, t ^ step) for t in range(count)])
+        step *= 2
+    return squares
 
 
 def per_device(hidden, down_weight, stream, norm_gain):
@@ -160,9 +171,10 @@
             tiled=True,
         )
     updated = stream[0].astype(F32) + projected
-    squares = total_squares(jnp.sum(updated * updated, axis=1), count)
-    scaled = updated * norm_gain[0].astype(F32)[None, :]
-    passed = lax.ppermute(scaled, "section", [(0, 1), (1, 0)])
+    squares = first_round(jnp.sum(updated * updated, axis=1), count)
+    gain = norm_gain[0].astype(F32)
+    passed = swapped(after(updated, squares) * gain[None, :])
+    squares = other_rounds(squares, count)
     inverse = lax.rsqrt(squares / full_width + 1e-05)
     normed = (passed * inverse[:, None]).astype(jnp.bfloat16)
     return (updated.astype(jnp.bfloat16)[None], normed[None])

time: 99.7 us -> 97.6 us (0.979)
  matrix products: 0 us -> 5.07 us
  Pallas kernels: 45 us -> 40.9 us
  waiting for transfers between devices: 19.5 us -> 17.3 us
  local copies, waits for them, and re-layouts: 1.9 us -> 0.02 us
  starting transfers between devices: 27 us -> 28 us
    dot_general x0 -> x1, matrix products: none -> 5.07 us  [reduce_line_of_four(): jnp.dot(hidden, lax.dynamic_slice_in_dim(weight, column * tile, tile, 1),...]
    pallas_call x6 -> x5, Pallas kernels: 45 us -> 40.9 us  [tile_products(): pl.pallas_call(kernel, out_shape=[jax.ShapeDtypeStruct((rows, n * tile),...]
    unnamed x6, local copies, waits for them, and re-layouts: 1.9 us -> 0.02 us
    ppermute x13, waiting for transfers between devices: 17.5 us -> 15.9 us  [send(): return lax.ppermute(block, 'tensor', pairs)]
    broadcast_in_dim x1 -> x2, other arithmetic: 1.03 us -> 2.02 us  [per_device(): return (updated.astype(jnp.bfloat16)[None], normed[None])]
  transfers between devices with their start and end apart: 16 -> 16, of which waited for: 7 -> 6; matrix products, arithmetic and copies ran while one was open for 2% -> 3% of each run, Pallas kernels for 41% -> 42%
where the time goes in v4:
time: 97.6 us; the launch traced here: 97.2 us
  Pallas kernels  40.9 us (42%)
  starting transfers between devices  28 us (29%)
  waiting for transfers between devices  17.3 us (18%)
  matrix products  5.07 us (5%)
  other arithmetic  4.98 us (5%)
    pallas_call x5, Pallas kernels, tile_products(): pl.pallas_call(kernel, out_shape=[jax.ShapeDtypeStruct((rows, n * tile),...  40.9 us
    ppermute x13, starting transfers between devices, send(): return lax.ppermute(block, 'tensor', pairs)  26.3 us
    ppermute x13, waiting for transfers between devices, send(): return lax.ppermute(block, 'tensor', pairs)  15.9 us
    dot_general x1, matrix products, reduce_line_of_four(): jnp.dot(hidden, lax.dynamic_slice_in_dim(weight, column * tile, tile, 1),...  5.07 us
    broadcast_in_dim x2, other arithmetic, per_device(): return (updated.astype(jnp.bfloat16)[None], normed[None])  2.02 us
    convert_element_type x9, other arithmetic, narrow(): return block.astype(WIRE)  1.97 us
  transfers between devices with their start and end apart: 16, of which 6 were waited for; matrix products, arithmetic and copies ran while one was open for 3% of the time, Pallas kernels for 42%

profile of v4, /device:TPU:0, one launch (start us, length us, event | category | flops | bytes accessed | tf_op | source)
XLA Modules:
  0.0 97.2 jit_solution(12845883546073338531)
XLA Ops:
  0.7 0.0 copy-start
  0.7 5.1 %fusion.6 = f16[384,512]{1,0:T(8,128)(2,1)S(1)} fusion(bf16[1,4096,8192]{2,1,0:T(8,128)(2,1)} %param.5, s32[]{:T(128)S(6)} %select_n.16, bf16[1,384,4096]{2,1,0:T(8,128)(2,1)} %param.4), kind=kOutput, calls=%fused_computation.12 | convolution fusion | flops 1610809344 | bytes 7733252 | tf_op jit(solution)/shard_map/dot_general | solution.py:103
  5.7 3.0 %collective-permute-start = (f16[384,512]{1,0:T(8,128)(2,1)S(1)}, f16[384,512]{1,0:T(8,128)(2,1)S(1)}, u32[]{:S(2)}, u32[]{:S(2)}) collective-permute-start(f16[384,512]{1,0:T(8,128)(2,1)S(1)} %fusion.6), channel_id=1, source_target_pairs={{0,2},{2,0},{4,6},{6,4},{8,10},{10,8},{12,14},{14,12},{1,3},{3,1},... | collective-permute-start | bytes 1179656 | tf_op jit(solution)/shard_map/ppermute | solution.py:65
  8.8 0.0 copy-done
  8.8 5.9 %tile_products.5 = (f32[384,512]{1,0:T(8,128)S(1)}, f32[384,512]{1,0:T(8,128)S(1)}) custom-call(s32[1]{0:T(128)} %bitcast.1.place_ref, bf16[384,4096]{1,0:T(8,128)(2,1)S(1)} %bitcast.23, bf16[4096,8192]{1,0:T(8,128)(2,1)} %bitcast.5.weight_ref), custom_call_target="tpu_custom_call" | custom-call | flops 3221225472 | bytes 9961472 | tf_op jit(solution)/shard_map/tile_products/pallas_call | solution.py:40
  14.7 0.1 convert_element_type.78
  14.8 0.1 collective-permute-start.1
  14.9 3.8 %collective-permute-done = f16[384,512]{1,0:T(8,128)(2,1)S(1)} collective-permute-done((f16[384,512]{1,0:T(8,128)(2,1)S(1)}, f16[384,512]{1,0:T(8,128)(2,1)S(1)}, u32[]{:S(2)}, u32[]{:S(2)}) %collective-permute-start) | collective-permute-done | bytes 393248 | tf_op jit(solution)/shard_map/ppermute | solution.py:65
  18.7 8.2 %tile_products.6 = (f32[384,1024]{1,0:T(8,128)S(1)}, f32[384,512]{1,0:T(8,128)S(1)}) custom-call(s32[1]{0:T(128)} %bitcast.1.place_ref, bf16[384,4096]{1,0:T(8,128)(2,1)S(1)} %bitcast.24, bf16[4096,8192]{1,0:T(8,128)(2,1)} %bitcast.5.weight_ref), custom_call_target="tpu_custom_call" | custom-call | flops 4831838208 | bytes 14942208 | tf_op jit(solution)/shard_map/tile_products/pallas_call | solution.py:40
  27.0 0.1 convert_element_type.79
  27.1 2.1 %collective-permute-start.2 = (f16[384,1024]{1,0:T(8,128)(2,1)S(1)}, f16[384,1024]{1,0:T(8,128)(2,1)S(1)}, u32[]{:S(2)}, u32[]{:S(2)}) collective-permute-start(f16[384,1024]{1,0:T(8,128)(2,1)S(1)} %convert_element_type.79), channel_id=1, source_target_pairs={{0,2},{2,0},{4,6},{6,4},{8,10},{10,8},{12,14},{14,12},{1,3},{3,1},... | collective-permute-start | bytes 2359304 | tf_op jit(solution)/shard_map/ppermute | solution.py:65
  29.2 0.0 collective-permute-done.1
  29.2 0.2 fusion.10
  29.5 3.5 %collective-permute-start.3 = (f16[384,1024]{1,0:T(8,128)(2,1)S(1)}, f16[384,1024]{1,0:T(8,128)(2,1)S(1)}, u32[]{:S(2)}, u32[]{:S(2)}) collective-permute-start(f16[384,1024]{1,0:T(8,128)(2,1)S(1)} %fusion.10), channel_id=1, source_target_pairs={{0,4},{2,6},{12,8},{14,10},{1,5},{3,7},{13,9},{15,11},{16,20},{18,... | collective-permute-start | bytes 2359304 | tf_op jit(solution)/shard_map/ppermute | solution.py:65
  33.0 10.3 %tile_products.7 = (f32[384,1024]{1,0:T(8,128)S(1)}, f32[384,1024]{1,0:T(8,128)S(1)}) custom-call(s32[1]{0:T(128)} %bitcast.1.place_ref, bf16[384,4096]{1,0:T(8,128)(2,1)S(1)} %bitcast.25, bf16[4096,8192]{1,0:T(8,128)(2,1)} %bitcast.5.weight_ref), custom_call_target="tpu_custom_call" | custom-call | flops 6442450944 | bytes 19922944 | tf_op jit(solution)/shard_map/tile_products/pallas_call | solution.py:40
  43.4 0.1 convert_element_type.82
  43.5 0.5 collective-permute-start.4
  44.0 2.7 %collective-permute-done.2 = f16[384,1024]{1,0:T(8,128)(2,1)S(1)} collective-permute-done((f16[384,1024]{1,0:T(8,128)(2,1)S(1)}, f16[384,1024]{1,0:T(8,128)(2,1)S(1)}, u32[]{:S(2)}, u32[]{:S(2)}) %collective-permute-start.2) | collective-permute-done | bytes 786464 | tf_op jit(solution)/shard_map/ppermute | solution.py:65
  46.7 0.3 fusion.9
  46.9 5.0 %collective-permute-start.5 = (f16[384,1024]{1,0:T(8,128)(2,1)S(1)}, f16[384,1024]{1,0:T(8,128)(2,1)S(1)}, u32[]{:S(2)}, u32[]{:S(2)}) collective-permute-start(f16[384,1024]{1,0:T(8,128)(2,1)S(1)} %fusion.9), channel_id=1, source_target_pairs={{0,4},{2,6},{12,8},{14,10},{1,5},{3,7},{13,9},{15,11},{16,20},{18,... | collective-permute-start | bytes 2359304 | tf_op jit(solution)/shard_map/ppermute | solution.py:65
  51.9 0.0 collective-permute-done.3
  51.9 0.4 add_convert_fusion.2
  52.3 1.3 %collective-permute-start.8 = (f16[384,1024]{1,0:T(8,128)(2,1)S(1)}, f16[384,1024]{1,0:T(8,128)(2,1)S(1)}, u32[]{:S(2)}, u32[]{:S(2)}) collective-permute-start(f16[384,1024]{1,0:T(8,128)(2,1)S(1)} %add_convert_fusion.2), channel_id=1, source_target_pairs={{4,12},{6,14},{8,0},{10,2},{5,13},{7,15},{9,1},{11,3},{20,28},{22,... | collective-permute-start | bytes 2359304 | tf_op jit(solution)/shard_map/ppermute | solution.py:65
  53.6 10.3 %tile_products.8 = (f32[384,1024]{1,0:T(8,128)S(1)}, f32[384,1024]{1,0:T(8,128)S(1)}) custom-call(s32[1]{0:T(128)} %bitcast.1.place_ref, bf16[384,4096]{1,0:T(8,128)(2,1)S(1)} %bitcast.26, bf16[4096,8192]{1,0:T(8,128)(2,1)} %bitcast.5.weight_ref), custom_call_target="tpu_custom_call" | custom-call | flops 6442450944 | bytes 19922944 | tf_op jit(solution)/shard_map/tile_products/pallas_call | solution.py:40
  63.9 0.1 convert_element_type.87
  64.1 1.7 %collective-permute-start.6 = (f16[384,1024]{1,0:T(8,128)(2,1)S(1)}, f16[384,1024]{1,0:T(8,128)(2,1)S(1)}, u32[]{:S(2)}, u32[]{:S(2)}) collective-permute-start(f16[384,1024]{1,0:T(8,128)(2,1)S(1)} %convert_element_type.87), channel_id=1, source_target_pairs={{0,2},{2,0},{4,6},{6,4},{8,10},{10,8},{12,14},{14,12},{1,3},{3,1},... | collective-permute-start | bytes 2359304 | tf_op jit(solution)/shard_map/ppermute | solution.py:65
  65.7 0.0 collective-permute-done.5
  65.7 0.4 add_convert_fusion.1
  66.2 0.0 collective-permute-done.4
  66.2 0.3 add_convert_fusion
  66.4 0.0 copy-start.1
  66.5 3.8 %collective-permute-start.7 = (f16[384,1024]{1,0:T(8,128)(2,1)S(1)}, f16[384,1024]{1,0:T(8,128)(2,1)S(1)}, u32[]{:S(2)}, u32[]{:S(2)}) collective-permute-start(f16[384,1024]{1,0:T(8,128)(2,1)S(1)} %add_convert_fusion), channel_id=1, source_target_pairs={{0,4},{2,6},{4,0},{6,2},{8,12},{10,14},{12,8},{14,10},{1,5},{3,7},... | collective-permute-start | bytes 2359304 | tf_op jit(solution)/shard_map/ppermute | solution.py:65
  70.2 0.9 collective-permute-start.9
  71.1 6.1 %tile_products.9 = f32[384,1024]{1,0:T(8,128)S(1)} custom-call(s32[1]{0:T(128)} %bitcast.1.place_ref, bf16[384,4096]{1,0:T(8,128)(2,1)S(1)} %bitcast.27, bf16[4096,8192]{1,0:T(8,128)(2,1)} %bitcast.5.weight_ref), custom_call_target="tpu_custom_call" | custom-call | flops 3221225472 | bytes 9961472 | tf_op jit(solution)/shard_map/tile_products/pallas_call | solution.py:40
  77.2 0.0 copy-start.2
  77.2 0.0 collective-permute-done.8
  77.2 1.6 %collective-permute-done.6 = f16[384,1024]{1,0:T(8,128)(2,1)S(1)} collective-permute-done((f16[384,1024]{1,0:T(8,128)(2,1)S(1)}, f16[384,1024]{1,0:T(8,128)(2,1)S(1)}, u32[]{:S(2)}, u32[]{:S(2)}) %collective-permute-start.6) | collective-permute-done | bytes 786464 | tf_op jit(solution)/shard_map/ppermute | solution.py:65
  78.8 6.2 %collective-permute-done.7 = f16[384,1024]{1,0:T(8,128)(2,1)S(1)} collective-permute-done((f16[384,1024]{1,0:T(8,128)(2,1)S(1)}, f16[384,1024]{1,0:T(8,128)(2,1)S(1)}, u32[]{:S(2)}, u32[]{:S(2)}) %collective-permute-start.7) | collective-permute-done | bytes 786464 | tf_op jit(solution)/shard_map/ppermute | solution.py:65
  85.0 0.0 collective-permute-done.9
  85.0 0.0 copy-done.1
  85.0 0.8 multiply_reduce_fusion
  85.8 0.1 collective-permute-start.11
  85.9 1.5 %collective-permute-start.10 = (f32[384]{0:T(512)S(1)}, f32[384]{0:T(512)S(1)}, u32[]{:S(2)}, u32[]{:S(2)}) collective-permute-start(f32[384]{0:T(512)S(1)} %get-tuple-element.40), channel_id=1, source_target_pairs={{0,1},{1,0},{2,3},{3,2},{4,5},{5,4},{6,7},{7,6},{8,9},{9,8},{10,11... | collective-permute-start | bytes 4616 | tf_op jit(solution)/shard_map/ppermute | solution.py:139
  87.4 0.0 copy-done.2
  87.4 1.5 %collective-permute-done.11 = f32[384]{0:T(512)S(1)} collective-permute-done((f32[384]{0:T(512)S(1)}, f32[384]{0:T(512)S(1)}, u32[]{:S(2)}, u32[]{:S(2)}) %collective-permute-start.11) | collective-permute-done | bytes 1568 | tf_op jit(solution)/shard_map/ppermute | solution.py:146
  88.9 0.0 collective-permute-done.10
  88.9 0.2 broadcast_multiply_fusion
  89.0 0.1 collective-permute-start.12
  89.1 2.5 %collective-permute-start.15 = (f32[384]{0:T(512)S(1)}, f32[384]{0:T(512)S(1)}, u32[]{:S(2)}, u32[]{:S(2)}) collective-permute-start(f32[384]{0:T(512)S(1)} %add.72), channel_id=1, source_target_pairs={{0,12},{2,14},{4,8},{6,10},{8,4},{10,6},{12,0},{14,2},{1,13},{3,15... | collective-permute-start | bytes 4616 | tf_op jit(solution)/shard_map/ppermute | solution.py:65
  91.7 0.0 collective-permute-start.14
  91.7 1.9 %collective-permute-start.13 = (f32[384]{0:T(512)S(1)}, f32[384]{0:T(512)S(1)}, u32[]{:S(2)}, u32[]{:S(2)}) collective-permute-start(f32[384]{0:T(512)S(1)} %add.72), channel_id=1, source_target_pairs={{0,4},{2,6},{4,0},{6,2},{8,12},{10,14},{12,8},{14,10},{1,5},{3,7},... | collective-permute-start | bytes 4616 | tf_op jit(solution)/shard_map/ppermute | solution.py:65
  93.6 1.0 %convert_bitcast_fusion = bf16[1,384,1024]{2,1,0:T(8,128)(2,1)} fusion(f32[384,1024]{1,0:T(8,128)S(1)} %get-tuple-element.39), kind=kLoop, calls=%fused_computation.18 | loop fusion | flops 393216 | bytes 2359296 | tf_op jit(solution)/shard_map/broadcast_in_dim | solution.py:180
  94.6 0.0 collective-permute-done.15
  94.6 1.6 %collective-permute-done.14 = f32[384]{0:T(512)S(1)} collective-permute-done((f32[384]{0:T(512)S(1)}, f32[384]{0:T(512)S(1)}, u32[]{:S(2)}, u32[]{:S(2)}) %collective-permute-start.14) | collective-permute-done | bytes 1568 | tf_op jit(solution)/shard_map/ppermute | solution.py:65
  96.1 0.0 collective-permute-done.13
  96.2 0.0 collective-permute-done.12
  96.2 1.0 %fusion.11 = bf16[1,384,1024]{2,1,0:T(8,128)(2,1)} fusion(f32[384,1024]{1,0:T(8,128)S(1)} %collective-permute-done.12, f32[384]{0:T(512)S(1)} %add_rsqrt_fusion), kind=kLoop, calls=%fused_computation.15 | loop fusion | flops 786432 | bytes 2360832 | tf_op jit(solution)/shard_map/broadcast_in_dim | solution.py:180
  (3 shorter events, 0.0 us)
Async XLA Ops:
  0.7 8.1 %copy-start = (bf16[1,384,4096]{2,1,0:T(8,128)(2,1)S(1)}, bf16[1,384,4096]{2,1,0:T(8,128)(2,1)}, u32[]{:S(2)}) copy-start(bf16[1,384,4096]{2,1,0:T(8,128)(2,1)} %param.4) | copy-start | bytes 9437188
  5.7 13.0 %collective-permute-start = (f16[384,512]{1,0:T(8,128)(2,1)S(1)}, f16[384,512]{1,0:T(8,128)(2,1)S(1)}, u32[]{:S(2)}, u32[]{:S(2)}) collective-permute-start(f16[384,512]{1,0:T(8,128)(2,1)S(1)} %fusion.6), channel_id=1, source_target_pairs={{0,2},{2,0},{4,6},{6,4},{8,10},{10,8},{12,14},{14,12},{1,3},{3,1},... | collective-permute-start | bytes 1179656 | tf_op jit(solution)/shard_map/ppermute | solution.py:65
  14.8 14.4 %collective-permute-start.1 = (f16[384,512]{1,0:T(8,128)(2,1)S(1)}, f16[384,512]{1,0:T(8,128)(2,1)S(1)}, u32[]{:S(2)}, u32[]{:S(2)}) collective-permute-start(f16[384,512]{1,0:T(8,128)(2,1)S(1)} %convert_element_type.78), channel_id=1, source_target_pairs={{0,2},{2,0},{4,6},{6,4},{8,10},{10,8},{12,14},{14,12},{1,3},{3,1},... | collective-permute-start | bytes 1179656 | tf_op jit(solution)/shard_map/ppermute | solution.py:65
  27.1 19.5 %collective-permute-start.2 = (f16[384,1024]{1,0:T(8,128)(2,1)S(1)}, f16[384,1024]{1,0:T(8,128)(2,1)S(1)}, u32[]{:S(2)}, u32[]{:S(2)}) collective-permute-start(f16[384,1024]{1,0:T(8,128)(2,1)S(1)} %convert_element_type.79), channel_id=1, source_target_pairs={{0,2},{2,0},{4,6},{6,4},{8,10},{10,8},{12,14},{14,12},{1,3},{3,1},... | collective-permute-start | bytes 2359304 | tf_op jit(solution)/shard_map/ppermute | solution.py:65
  29.5 22.4 %collective-permute-start.3 = (f16[384,1024]{1,0:T(8,128)(2,1)S(1)}, f16[384,1024]{1,0:T(8,128)(2,1)S(1)}, u32[]{:S(2)}, u32[]{:S(2)}) collective-permute-start(f16[384,1024]{1,0:T(8,128)(2,1)S(1)} %fusion.10), channel_id=1, source_target_pairs={{0,4},{2,6},{12,8},{14,10},{1,5},{3,7},{13,9},{15,11},{16,20},{18,... | collective-permute-start | bytes 2359304 | tf_op jit(solution)/shard_map/ppermute | solution.py:65
  43.5 22.7 %collective-permute-start.4 = (f16[384,1024]{1,0:T(8,128)(2,1)S(1)}, f16[384,1024]{1,0:T(8,128)(2,1)S(1)}, u32[]{:S(2)}, u32[]{:S(2)}) collective-permute-start(f16[384,1024]{1,0:T(8,128)(2,1)S(1)} %convert_element_type.82), channel_id=1, source_target_pairs={{0,2},{2,0},{4,6},{6,4},{8,10},{10,8},{12,14},{14,12},{1,3},{3,1},... | collective-permute-start | bytes 2359304 | tf_op jit(solution)/shard_map/ppermute | solution.py:65
  46.9 18.8 %collective-permute-start.5 = (f16[384,1024]{1,0:T(8,128)(2,1)S(1)}, f16[384,1024]{1,0:T(8,128)(2,1)S(1)}, u32[]{:S(2)}, u32[]{:S(2)}) collective-permute-start(f16[384,1024]{1,0:T(8,128)(2,1)S(1)} %fusion.9), channel_id=1, source_target_pairs={{0,4},{2,6},{12,8},{14,10},{1,5},{3,7},{13,9},{15,11},{16,20},{18,... | collective-permute-start | bytes 2359304 | tf_op jit(solution)/shard_map/ppermute | solution.py:65
  52.3 24.9 %collective-permute-start.8 = (f16[384,1024]{1,0:T(8,128)(2,1)S(1)}, f16[384,1024]{1,0:T(8,128)(2,1)S(1)}, u32[]{:S(2)}, u32[]{:S(2)}) collective-permute-start(f16[384,1024]{1,0:T(8,128)(2,1)S(1)} %add_convert_fusion.2), channel_id=1, source_target_pairs={{4,12},{6,14},{8,0},{10,2},{5,13},{7,15},{9,1},{11,3},{20,28},{22,... | collective-permute-start | bytes 2359304 | tf_op jit(solution)/shard_map/ppermute | solution.py:65
  64.1 14.7 %collective-permute-start.6 = (f16[384,1024]{1,0:T(8,128)(2,1)S(1)}, f16[384,1024]{1,0:T(8,128)(2,1)S(1)}, u32[]{:S(2)}, u32[]{:S(2)}) collective-permute-start(f16[384,1024]{1,0:T(8,128)(2,1)S(1)} %convert_element_type.87), channel_id=1, source_target_pairs={{0,2},{2,0},{4,6},{6,4},{8,10},{10,8},{12,14},{14,12},{1,3},{3,1},... | collective-permute-start | bytes 2359304 | tf_op jit(solution)/shard_map/ppermute | solution.py:65
  66.4 18.5 %copy-start.1 = (bf16[1,384,1024]{2,1,0:T(8,128)(2,1)S(1)}, bf16[1,384,1024]{2,1,0:T(8,128)(2,1)}, u32[]{:S(2)}) copy-start(bf16[1,384,1024]{2,1,0:T(8,128)(2,1)} %param.6) | copy-start | bytes 2359300
  66.5 18.5 %collective-permute-start.7 = (f16[384,1024]{1,0:T(8,128)(2,1)S(1)}, f16[384,1024]{1,0:T(8,128)(2,1)S(1)}, u32[]{:S(2)}, u32[]{:S(2)}) collective-permute-start(f16[384,1024]{1,0:T(8,128)(2,1)S(1)} %add_convert_fusion), channel_id=1, source_target_pairs={{0,4},{2,6},{4,0},{6,2},{8,12},{10,14},{12,8},{14,10},{1,5},{3,7},... | collective-permute-start | bytes 2359304 | tf_op jit(solution)/shard_map/ppermute | solution.py:65
  70.2 14.8 %collective-permute-start.9 = (f16[384,1024]{1,0:T(8,128)(2,1)S(1)}, f16[384,1024]{1,0:T(8,128)(2,1)S(1)}, u32[]{:S(2)}, u32[]{:S(2)}) collective-permute-start(f16[384,1024]{1,0:T(8,128)(2,1)S(1)} %add_convert_fusion.1), channel_id=1, source_target_pairs={{4,8},{6,10},{8,4},{10,6},{5,9},{7,11},{9,5},{11,7},{20,24},{22,26... | collective-permute-start | bytes 2359304 | tf_op jit(solution)/shard_map/ppermute | solution.py:65
  77.2 10.2 %copy-start.2 = (bf16[1,1024]{1,0:T(2,128)(2,1)S(1)}, bf16[1,1024]{1,0:T(2,128)(2,1)}, u32[]{:S(2)}) copy-start(bf16[1,1024]{1,0:T(2,128)(2,1)} %param.7) | copy-start | bytes 6148
  85.8 3.1 %collective-permute-start.11 = (f32[384]{0:T(512)S(1)}, f32[384]{0:T(512)S(1)}, u32[]{:S(2)}, u32[]{:S(2)}) collective-permute-start(f32[384]{0:T(512)S(1)} %get-tuple-element.40), channel_id=1, source_target_pairs={{0,3},{1,2},{2,1},{3,0},{4,7},{5,6},{6,5},{7,4},{8,11},{9,10},{10,... | collective-permute-start | bytes 4616 | tf_op jit(solution)/shard_map/ppermute | solution.py:146
  85.9 3.0 %collective-permute-start.10 = (f32[384]{0:T(512)S(1)}, f32[384]{0:T(512)S(1)}, u32[]{:S(2)}, u32[]{:S(2)}) collective-permute-start(f32[384]{0:T(512)S(1)} %get-tuple-element.40), channel_id=1, source_target_pairs={{0,1},{1,0},{2,3},{3,2},{4,5},{5,4},{6,7},{7,6},{8,9},{9,8},{10,11... | collective-permute-start | bytes 4616 | tf_op jit(solution)/shard_map/ppermute | solution.py:139
  89.0 7.1 %collective-permute-start.12 = (f32[384,1024]{1,0:T(8,128)S(1)}, f32[384,1024]{1,0:T(8,128)S(1)}, u32[]{:S(2)}, u32[]{:S(2)}) collective-permute-start(f32[384,1024]{1,0:T(8,128)S(1)} %broadcast_multiply_fusion), channel_id=1, source_target_pairs={{0,1},{1,0},{2,3},{3,2},{4,5},{5,4},{6,7},{7,6},{8,9},{9,8},{10,11... | collective-permute-start | bytes 4718600 | tf_op jit(solution)/shard_map/ppermute | solution.py:139
  89.1 5.4 %collective-permute-start.15 = (f32[384]{0:T(512)S(1)}, f32[384]{0:T(512)S(1)}, u32[]{:S(2)}, u32[]{:S(2)}) collective-permute-start(f32[384]{0:T(512)S(1)} %add.72), channel_id=1, source_target_pairs={{0,12},{2,14},{4,8},{6,10},{8,4},{10,6},{12,0},{14,2},{1,13},{3,15... | collective-permute-start | bytes 4616 | tf_op jit(solution)/shard_map/ppermute | solution.py:65
  91.7 4.5 %collective-permute-start.14 = (f32[384]{0:T(512)S(1)}, f32[384]{0:T(512)S(1)}, u32[]{:S(2)}, u32[]{:S(2)}) collective-permute-start(f32[384]{0:T(512)S(1)} %add.72), channel_id=1, source_target_pairs={{0,8},{2,10},{4,12},{6,14},{8,0},{10,2},{12,4},{14,6},{1,9},{3,11}... | collective-permute-start | bytes 4616 | tf_op jit(solution)/shard_map/ppermute | solution.py:65
  91.7 4.5 %collective-permute-start.13 = (f32[384]{0:T(512)S(1)}, f32[384]{0:T(512)S(1)}, u32[]{:S(2)}, u32[]{:S(2)}) collective-permute-start(f32[384]{0:T(512)S(1)} %add.72), channel_id=1, source_target_pairs={{0,4},{2,6},{4,0},{6,2},{8,12},{10,14},{12,8},{14,10},{1,5},{3,7},... | collective-permute-start | bytes 4616 | tf_op jit(solution)/shard_map/ppermute | solution.py:65

commit v5 on v4

--- a/solution.py
+++ b/solution.py
@@ -51,7 +51,7 @@
                 pl.BlockSpec((rows, tile), out_tile(s, n)) for s, n in zip(starts, counts)
             ],
         ),
-        compiler_params=pltpu.CompilerParams(vmem_limit_bytes=32 * 2**20),
+        compiler_params=pltpu.CompilerParams(vmem_limit_bytes=24 * 2**20),
         cost_estimate=pl.CostEstimate(
             flops=2 * rows * depth * tile * len(listed),
             bytes_accessed=(2 * depth + 4 * rows) * tile * len(listed),

time: 97.6 us -> 97.6 us (level)
  no operation moved by 1% of the time
where the time goes in v5:
time: 97.6 us; the launch traced here: 97.2 us
  Pallas kernels  40.9 us (42%)
  starting transfers between devices  28 us (29%)
  waiting for transfers between devices  17.3 us (18%)
  matrix products  5.07 us (5%)
  other arithmetic  4.98 us (5%)
    pallas_call x5, Pallas kernels, tile_products(): pl.pallas_call(kernel, out_shape=[jax.ShapeDtypeStruct((rows, n * tile),...  40.9 us
    ppermute x13, starting transfers between devices, send(): return lax.ppermute(block, 'tensor', pairs)  26.3 us
    ppermute x13, waiting for transfers between devices, send(): return lax.ppermute(block, 'tensor', pairs)  15.9 us
    dot_general x1, matrix products, reduce_line_of_four(): jnp.dot(hidden, lax.dynamic_slice_in_dim(weight, column * tile, tile, 1),...  5.07 us
    broadcast_in_dim x2, other arithmetic, per_device(): return (updated.astype(jnp.bfloat16)[None], normed[None])  2.02 us
    convert_element_type x9, other arithmetic, narrow(): return block.astype(WIRE)  1.97 us
  transfers between devices with their start and end apart: 16, of which 6 were waited for; matrix products, arithmetic and copies ran while one was open for 3% of the time, Pallas kernels for 42%

profile of v5, /device:TPU:0, one launch (start us, length us, event | category | flops | bytes accessed | tf_op | source)
XLA Modules:
  0.0 97.2 jit_solution(13505114121397130072)
XLA Ops:
  0.7 0.0 copy-start
  0.7 5.1 %fusion.6 = f16[384,512]{1,0:T(8,128)(2,1)S(1)} fusion(bf16[1,4096,8192]{2,1,0:T(8,128)(2,1)} %param.5, s32[]{:T(128)S(6)} %select_n.16, bf16[1,384,4096]{2,1,0:T(8,128)(2,1)} %param.4), kind=kOutput, calls=%fused_computation.12 | convolution fusion | flops 1610809344 | bytes 7733252 | tf_op jit(solution)/shard_map/dot_general | solution.py:103
  5.7 3.0 %collective-permute-start = (f16[384,512]{1,0:T(8,128)(2,1)S(1)}, f16[384,512]{1,0:T(8,128)(2,1)S(1)}, u32[]{:S(2)}, u32[]{:S(2)}) collective-permute-start(f16[384,512]{1,0:T(8,128)(2,1)S(1)} %fusion.6), channel_id=1, source_target_pairs={{0,2},{2,0},{4,6},{6,4},{8,10},{10,8},{12,14},{14,12},{1,3},{3,1},... | collective-permute-start | bytes 1179656 | tf_op jit(solution)/shard_map/ppermute | solution.py:65
  8.8 0.0 copy-done
  8.8 5.9 %tile_products.5 = (f32[384,512]{1,0:T(8,128)S(1)}, f32[384,512]{1,0:T(8,128)S(1)}) custom-call(s32[1]{0:T(128)} %bitcast.1.place_ref, bf16[384,4096]{1,0:T(8,128)(2,1)S(1)} %bitcast.23, bf16[4096,8192]{1,0:T(8,128)(2,1)} %bitcast.5.weight_ref), custom_call_target="tpu_custom_call" | custom-call | flops 3221225472 | bytes 9961472 | tf_op jit(solution)/shard_map/tile_products/pallas_call | solution.py:40
  14.7 0.1 convert_element_type.78
  14.8 0.1 collective-permute-start.1
  14.9 3.8 %collective-permute-done = f16[384,512]{1,0:T(8,128)(2,1)S(1)} collective-permute-done((f16[384,512]{1,0:T(8,128)(2,1)S(1)}, f16[384,512]{1,0:T(8,128)(2,1)S(1)}, u32[]{:S(2)}, u32[]{:S(2)}) %collective-permute-start) | collective-permute-done | bytes 393248 | tf_op jit(solution)/shard_map/ppermute | solution.py:65
  18.7 8.2 %tile_products.6 = (f32[384,1024]{1,0:T(8,128)S(1)}, f32[384,512]{1,0:T(8,128)S(1)}) custom-call(s32[1]{0:T(128)} %bitcast.1.place_ref, bf16[384,4096]{1,0:T(8,128)(2,1)S(1)} %bitcast.24, bf16[4096,8192]{1,0:T(8,128)(2,1)} %bitcast.5.weight_ref), custom_call_target="tpu_custom_call" | custom-call | flops 4831838208 | bytes 14942208 | tf_op jit(solution)/shard_map/tile_products/pallas_call | solution.py:40
  27.0 0.1 convert_element_type.79
  27.1 2.1 %collective-permute-start.2 = (f16[384,1024]{1,0:T(8,128)(2,1)S(1)}, f16[384,1024]{1,0:T(8,128)(2,1)S(1)}, u32[]{:S(2)}, u32[]{:S(2)}) collective-permute-start(f16[384,1024]{1,0:T(8,128)(2,1)S(1)} %convert_element_type.79), channel_id=1, source_target_pairs={{0,2},{2,0},{4,6},{6,4},{8,10},{10,8},{12,14},{14,12},{1,3},{3,1},... | collective-permute-start | bytes 2359304 | tf_op jit(solution)/shard_map/ppermute | solution.py:65
  29.2 0.0 collective-permute-done.1
  29.2 0.2 fusion.10
  29.5 3.5 %collective-permute-start.3 = (f16[384,1024]{1,0:T(8,128)(2,1)S(1)}, f16[384,1024]{1,0:T(8,128)(2,1)S(1)}, u32[]{:S(2)}, u32[]{:S(2)}) collective-permute-start(f16[384,1024]{1,0:T(8,128)(2,1)S(1)} %fusion.10), channel_id=1, source_target_pairs={{0,4},{2,6},{12,8},{14,10},{1,5},{3,7},{13,9},{15,11},{16,20},{18,... | collective-permute-start | bytes 2359304 | tf_op jit(solution)/shard_map/ppermute | solution.py:65
  33.0 10.3 %tile_products.7 = (f32[384,1024]{1,0:T(8,128)S(1)}, f32[384,1024]{1,0:T(8,128)S(1)}) custom-call(s32[1]{0:T(128)} %bitcast.1.place_ref, bf16[384,4096]{1,0:T(8,128)(2,1)S(1)} %bitcast.25, bf16[4096,8192]{1,0:T(8,128)(2,1)} %bitcast.5.weight_ref), custom_call_target="tpu_custom_call" | custom-call | flops 6442450944 | bytes 19922944 | tf_op jit(solution)/shard_map/tile_products/pallas_call | solution.py:40
  43.4 0.1 convert_element_type.82
  43.5 0.5 collective-permute-start.4
  44.0 2.7 %collective-permute-done.2 = f16[384,1024]{1,0:T(8,128)(2,1)S(1)} collective-permute-done((f16[384,1024]{1,0:T(8,128)(2,1)S(1)}, f16[384,1024]{1,0:T(8,128)(2,1)S(1)}, u32[]{:S(2)}, u32[]{:S(2)}) %collective-permute-start.2) | collective-permute-done | bytes 786464 | tf_op jit(solution)/shard_map/ppermute | solution.py:65
  46.7 0.3 fusion.9
  46.9 5.0 %collective-permute-start.5 = (f16[384,1024]{1,0:T(8,128)(2,1)S(1)}, f16[384,1024]{1,0:T(8,128)(2,1)S(1)}, u32[]{:S(2)}, u32[]{:S(2)}) collective-permute-start(f16[384,1024]{1,0:T(8,128)(2,1)S(1)} %fusion.9), channel_id=1, source_target_pairs={{0,4},{2,6},{12,8},{14,10},{1,5},{3,7},{13,9},{15,11},{16,20},{18,... | collective-permute-start | bytes 2359304 | tf_op jit(solution)/shard_map/ppermute | solution.py:65
  51.9 0.0 collective-permute-done.3
  51.9 0.4 add_convert_fusion.2
  52.3 1.3 %collective-permute-start.8 = (f16[384,1024]{1,0:T(8,128)(2,1)S(1)}, f16[384,1024]{1,0:T(8,128)(2,1)S(1)}, u32[]{:S(2)}, u32[]{:S(2)}) collective-permute-start(f16[384,1024]{1,0:T(8,128)(2,1)S(1)} %add_convert_fusion.2), channel_id=1, source_target_pairs={{4,12},{6,14},{8,0},{10,2},{5,13},{7,15},{9,1},{11,3},{20,28},{22,... | collective-permute-start | bytes 2359304 | tf_op jit(solution)/shard_map/ppermute | solution.py:65
  53.6 10.3 %tile_products.8 = (f32[384,1024]{1,0:T(8,128)S(1)}, f32[384,1024]{1,0:T(8,128)S(1)}) custom-call(s32[1]{0:T(128)} %bitcast.1.place_ref, bf16[384,4096]{1,0:T(8,128)(2,1)S(1)} %bitcast.26, bf16[4096,8192]{1,0:T(8,128)(2,1)} %bitcast.5.weight_ref), custom_call_target="tpu_custom_call" | custom-call | flops 6442450944 | bytes 19922944 | tf_op jit(solution)/shard_map/tile_products/pallas_call | solution.py:40
  63.9 0.1 convert_element_type.87
  64.1 1.7 %collective-permute-start.6 = (f16[384,1024]{1,0:T(8,128)(2,1)S(1)}, f16[384,1024]{1,0:T(8,128)(2,1)S(1)}, u32[]{:S(2)}, u32[]{:S(2)}) collective-permute-start(f16[384,1024]{1,0:T(8,128)(2,1)S(1)} %convert_element_type.87), channel_id=1, source_target_pairs={{0,2},{2,0},{4,6},{6,4},{8,10},{10,8},{12,14},{14,12},{1,3},{3,1},... | collective-permute-start | bytes 2359304 | tf_op jit(solution)/shard_map/ppermute | solution.py:65
  65.7 0.0 collective-permute-done.5
  65.7 0.4 add_convert_fusion.1
  66.2 0.0 collective-permute-done.4
  66.2 0.3 add_convert_fusion
  66.4 0.0 copy-start.1
  66.5 3.8 %collective-permute-start.7 = (f16[384,1024]{1,0:T(8,128)(2,1)S(1)}, f16[384,1024]{1,0:T(8,128)(2,1)S(1)}, u32[]{:S(2)}, u32[]{:S(2)}) collective-permute-start(f16[384,1024]{1,0:T(8,128)(2,1)S(1)} %add_convert_fusion), channel_id=1, source_target_pairs={{0,4},{2,6},{4,0},{6,2},{8,12},{10,14},{12,8},{14,10},{1,5},{3,7},... | collective-permute-start | bytes 2359304 | tf_op jit(solution)/shard_map/ppermute | solution.py:65
  70.2 0.9 collective-permute-start.9
  71.1 6.1 %tile_products.9 = f32[384,1024]{1,0:T(8,128)S(1)} custom-call(s32[1]{0:T(128)} %bitcast.1.place_ref, bf16[384,4096]{1,0:T(8,128)(2,1)S(1)} %bitcast.27, bf16[4096,8192]{1,0:T(8,128)(2,1)} %bitcast.5.weight_ref), custom_call_target="tpu_custom_call" | custom-call | flops 3221225472 | bytes 9961472 | tf_op jit(solution)/shard_map/tile_products/pallas_call | solution.py:40
  77.2 0.0 copy-start.2
  77.2 0.0 collective-permute-done.8
  77.2 1.6 %collective-permute-done.6 = f16[384,1024]{1,0:T(8,128)(2,1)S(1)} collective-permute-done((f16[384,1024]{1,0:T(8,128)(2,1)S(1)}, f16[384,1024]{1,0:T(8,128)(2,1)S(1)}, u32[]{:S(2)}, u32[]{:S(2)}) %collective-permute-start.6) | collective-permute-done | bytes 786464 | tf_op jit(solution)/shard_map/ppermute | solution.py:65
  78.8 6.2 %collective-permute-done.7 = f16[384,1024]{1,0:T(8,128)(2,1)S(1)} collective-permute-done((f16[384,1024]{1,0:T(8,128)(2,1)S(1)}, f16[384,1024]{1,0:T(8,128)(2,1)S(1)}, u32[]{:S(2)}, u32[]{:S(2)}) %collective-permute-start.7) | collective-permute-done | bytes 786464 | tf_op jit(solution)/shard_map/ppermute | solution.py:65
  85.0 0.0 collective-permute-done.9
  85.0 0.0 copy-done.1
  85.0 0.8 multiply_reduce_fusion
  85.8 0.1 collective-permute-start.11
  85.9 1.5 %collective-permute-start.10 = (f32[384]{0:T(512)S(1)}, f32[384]{0:T(512)S(1)}, u32[]{:S(2)}, u32[]{:S(2)}) collective-permute-start(f32[384]{0:T(512)S(1)} %get-tuple-element.40), channel_id=1, source_target_pairs={{0,1},{1,0},{2,3},{3,2},{4,5},{5,4},{6,7},{7,6},{8,9},{9,8},{10,11... | collective-permute-start | bytes 4616 | tf_op jit(solution)/shard_map/ppermute | solution.py:139
  87.4 0.0 copy-done.2
  87.4 1.5 %collective-permute-done.11 = f32[384]{0:T(512)S(1)} collective-permute-done((f32[384]{0:T(512)S(1)}, f32[384]{0:T(512)S(1)}, u32[]{:S(2)}, u32[]{:S(2)}) %collective-permute-start.11) | collective-permute-done | bytes 1568 | tf_op jit(solution)/shard_map/ppermute | solution.py:146
  88.9 0.0 collective-permute-done.10
  88.9 0.2 broadcast_multiply_fusion
  89.0 0.1 collective-permute-start.12
  89.1 2.5 %collective-permute-start.15 = (f32[384]{0:T(512)S(1)}, f32[384]{0:T(512)S(1)}, u32[]{:S(2)}, u32[]{:S(2)}) collective-permute-start(f32[384]{0:T(512)S(1)} %add.72), channel_id=1, source_target_pairs={{0,12},{2,14},{4,8},{6,10},{8,4},{10,6},{12,0},{14,2},{1,13},{3,15... | collective-permute-start | bytes 4616 | tf_op jit(solution)/shard_map/ppermute | solution.py:65
  91.7 0.0 collective-permute-start.14
  91.7 1.9 %collective-permute-start.13 = (f32[384]{0:T(512)S(1)}, f32[384]{0:T(512)S(1)}, u32[]{:S(2)}, u32[]{:S(2)}) collective-permute-start(f32[384]{0:T(512)S(1)} %add.72), channel_id=1, source_target_pairs={{0,4},{2,6},{4,0},{6,2},{8,12},{10,14},{12,8},{14,10},{1,5},{3,7},... | collective-permute-start | bytes 4616 | tf_op jit(solution)/shard_map/ppermute | solution.py:65
  93.6 1.0 %convert_bitcast_fusion = bf16[1,384,1024]{2,1,0:T(8,128)(2,1)} fusion(f32[384,1024]{1,0:T(8,128)S(1)} %get-tuple-element.39), kind=kLoop, calls=%fused_computation.18 | loop fusion | flops 393216 | bytes 2359296 | tf_op jit(solution)/shard_map/broadcast_in_dim | solution.py:180
  94.6 0.0 collective-permute-done.15
  94.6 1.6 %collective-permute-done.14 = f32[384]{0:T(512)S(1)} collective-permute-done((f32[384]{0:T(512)S(1)}, f32[384]{0:T(512)S(1)}, u32[]{:S(2)}, u32[]{:S(2)}) %collective-permute-start.14) | collective-permute-done | bytes 1568 | tf_op jit(solution)/shard_map/ppermute | solution.py:65
  96.1 0.0 collective-permute-done.13
  96.2 0.0 collective-permute-done.12
  96.2 1.0 %fusion.11 = bf16[1,384,1024]{2,1,0:T(8,128)(2,1)} fusion(f32[384,1024]{1,0:T(8,128)S(1)} %collective-permute-done.12, f32[384]{0:T(512)S(1)} %add_rsqrt_fusion), kind=kLoop, calls=%fused_computation.15 | loop fusion | flops 786432 | bytes 2360832 | tf_op jit(solution)/shard_map/broadcast_in_dim | solution.py:180
  (3 shorter events, 0.0 us)
Async XLA Ops:
  0.7 8.1 %copy-start = (bf16[1,384,4096]{2,1,0:T(8,128)(2,1)S(1)}, bf16[1,384,4096]{2,1,0:T(8,128)(2,1)}, u32[]{:S(2)}) copy-start(bf16[1,384,4096]{2,1,0:T(8,128)(2,1)} %param.4) | copy-start | bytes 9437188
  5.7 13.0 %collective-permute-start = (f16[384,512]{1,0:T(8,128)(2,1)S(1)}, f16[384,512]{1,0:T(8,128)(2,1)S(1)}, u32[]{:S(2)}, u32[]{:S(2)}) collective-permute-start(f16[384,512]{1,0:T(8,128)(2,1)S(1)} %fusion.6), channel_id=1, source_target_pairs={{0,2},{2,0},{4,6},{6,4},{8,10},{10,8},{12,14},{14,12},{1,3},{3,1},... | collective-permute-start | bytes 1179656 | tf_op jit(solution)/shard_map/ppermute | solution.py:65
  14.8 14.4 %collective-permute-start.1 = (f16[384,512]{1,0:T(8,128)(2,1)S(1)}, f16[384,512]{1,0:T(8,128)(2,1)S(1)}, u32[]{:S(2)}, u32[]{:S(2)}) collective-permute-start(f16[384,512]{1,0:T(8,128)(2,1)S(1)} %convert_element_type.78), channel_id=1, source_target_pairs={{0,2},{2,0},{4,6},{6,4},{8,10},{10,8},{12,14},{14,12},{1,3},{3,1},... | collective-permute-start | bytes 1179656 | tf_op jit(solution)/shard_map/ppermute | solution.py:65
  27.1 19.5 %collective-permute-start.2 = (f16[384,1024]{1,0:T(8,128)(2,1)S(1)}, f16[384,1024]{1,0:T(8,128)(2,1)S(1)}, u32[]{:S(2)}, u32[]{:S(2)}) collective-permute-start(f16[384,1024]{1,0:T(8,128)(2,1)S(1)} %convert_element_type.79), channel_id=1, source_target_pairs={{0,2},{2,0},{4,6},{6,4},{8,10},{10,8},{12,14},{14,12},{1,3},{3,1},... | collective-permute-start | bytes 2359304 | tf_op jit(solution)/shard_map/ppermute | solution.py:65
  29.5 22.4 %collective-permute-start.3 = (f16[384,1024]{1,0:T(8,128)(2,1)S(1)}, f16[384,1024]{1,0:T(8,128)(2,1)S(1)}, u32[]{:S(2)}, u32[]{:S(2)}) collective-permute-start(f16[384,1024]{1,0:T(8,128)(2,1)S(1)} %fusion.10), channel_id=1, source_target_pairs={{0,4},{2,6},{12,8},{14,10},{1,5},{3,7},{13,9},{15,11},{16,20},{18,... | collective-permute-start | bytes 2359304 | tf_op jit(solution)/shard_map/ppermute | solution.py:65
  43.5 22.7 %collective-permute-start.4 = (f16[384,1024]{1,0:T(8,128)(2,1)S(1)}, f16[384,1024]{1,0:T(8,128)(2,1)S(1)}, u32[]{:S(2)}, u32[]{:S(2)}) collective-permute-start(f16[384,1024]{1,0:T(8,128)(2,1)S(1)} %convert_element_type.82), channel_id=1, source_target_pairs={{0,2},{2,0},{4,6},{6,4},{8,10},{10,8},{12,14},{14,12},{1,3},{3,1},... | collective-permute-start | bytes 2359304 | tf_op jit(solution)/shard_map/ppermute | solution.py:65
  46.9 18.8 %collective-permute-start.5 = (f16[384,1024]{1,0:T(8,128)(2,1)S(1)}, f16[384,1024]{1,0:T(8,128)(2,1)S(1)}, u32[]{:S(2)}, u32[]{:S(2)}) collective-permute-start(f16[384,1024]{1,0:T(8,128)(2,1)S(1)} %fusion.9), channel_id=1, source_target_pairs={{0,4},{2,6},{12,8},{14,10},{1,5},{3,7},{13,9},{15,11},{16,20},{18,... | collective-permute-start | bytes 2359304 | tf_op jit(solution)/shard_map/ppermute | solution.py:65
  52.3 24.9 %collective-permute-start.8 = (f16[384,1024]{1,0:T(8,128)(2,1)S(1)}, f16[384,1024]{1,0:T(8,128)(2,1)S(1)}, u32[]{:S(2)}, u32[]{:S(2)}) collective-permute-start(f16[384,1024]{1,0:T(8,128)(2,1)S(1)} %add_convert_fusion.2), channel_id=1, source_target_pairs={{4,12},{6,14},{8,0},{10,2},{5,13},{7,15},{9,1},{11,3},{20,28},{22,... | collective-permute-start | bytes 2359304 | tf_op jit(solution)/shard_map/ppermute | solution.py:65
  64.1 14.7 %collective-permute-start.6 = (f16[384,1024]{1,0:T(8,128)(2,1)S(1)}, f16[384,1024]{1,0:T(8,128)(2,1)S(1)}, u32[]{:S(2)}, u32[]{:S(2)}) collective-permute-start(f16[384,1024]{1,0:T(8,128)(2,1)S(1)} %convert_element_type.87), channel_id=1, source_target_pairs={{0,2},{2,0},{4,6},{6,4},{8,10},{10,8},{12,14},{14,12},{1,3},{3,1},... | collective-permute-start | bytes 2359304 | tf_op jit(solution)/shard_map/ppermute | solution.py:65
  66.4 18.5 %copy-start.1 = (bf16[1,384,1024]{2,1,0:T(8,128)(2,1)S(1)}, bf16[1,384,1024]{2,1,0:T(8,128)(2,1)}, u32[]{:S(2)}) copy-start(bf16[1,384,1024]{2,1,0:T(8,128)(2,1)} %param.6) | copy-start | bytes 2359300
  66.5 18.5 %collective-permute-start.7 = (f16[384,1024]{1,0:T(8,128)(2,1)S(1)}, f16[384,1024]{1,0:T(8,128)(2,1)S(1)}, u32[]{:S(2)}, u32[]{:S(2)}) collective-permute-start(f16[384,1024]{1,0:T(8,128)(2,1)S(1)} %add_convert_fusion), channel_id=1, source_target_pairs={{0,4},{2,6},{4,0},{6,2},{8,12},{10,14},{12,8},{14,10},{1,5},{3,7},... | collective-permute-start | bytes 2359304 | tf_op jit(solution)/shard_map/ppermute | solution.py:65
  70.2 14.8 %collective-permute-start.9 = (f16[384,1024]{1,0:T(8,128)(2,1)S(1)}, f16[384,1024]{1,0:T(8,128)(2,1)S(1)}, u32[]{:S(2)}, u32[]{:S(2)}) collective-permute-start(f16[384,1024]{1,0:T(8,128)(2,1)S(1)} %add_convert_fusion.1), channel_id=1, source_target_pairs={{4,8},{6,10},{8,4},{10,6},{5,9},{7,11},{9,5},{11,7},{20,24},{22,26... | collective-permute-start | bytes 2359304 | tf_op jit(solution)/shard_map/ppermute | solution.py:65
  77.2 10.2 %copy-start.2 = (bf16[1,1024]{1,0:T(2,128)(2,1)S(1)}, bf16[1,1024]{1,0:T(2,128)(2,1)}, u32[]{:S(2)}) copy-start(bf16[1,1024]{1,0:T(2,128)(2,1)} %param.7) | copy-start | bytes 6148
  85.8 3.1 %collective-permute-start.11 = (f32[384]{0:T(512)S(1)}, f32[384]{0:T(512)S(1)}, u32[]{:S(2)}, u32[]{:S(2)}) collective-permute-start(f32[384]{0:T(512)S(1)} %get-tuple-element.40), channel_id=1, source_target_pairs={{0,3},{1,2},{2,1},{3,0},{4,7},{5,6},{6,5},{7,4},{8,11},{9,10},{10,... | collective-permute-start | bytes 4616 | tf_op jit(solution)/shard_map/ppermute | solution.py:146
  85.9 3.0 %collective-permute-start.10 = (f32[384]{0:T(512)S(1)}, f32[384]{0:T(512)S(1)}, u32[]{:S(2)}, u32[]{:S(2)}) collective-permute-start(f32[384]{0:T(512)S(1)} %get-tuple-element.40), channel_id=1, source_target_pairs={{0,1},{1,0},{2,3},{3,2},{4,5},{5,4},{6,7},{7,6},{8,9},{9,8},{10,11... | collective-permute-start | bytes 4616 | tf_op jit(solution)/shard_map/ppermute | solution.py:139
  89.0 7.1 %collective-permute-start.12 = (f32[384,1024]{1,0:T(8,128)S(1)}, f32[384,1024]{1,0:T(8,128)S(1)}, u32[]{:S(2)}, u32[]{:S(2)}) collective-permute-start(f32[384,1024]{1,0:T(8,128)S(1)} %broadcast_multiply_fusion), channel_id=1, source_target_pairs={{0,1},{1,0},{2,3},{3,2},{4,5},{5,4},{6,7},{7,6},{8,9},{9,8},{10,11... | collective-permute-start | bytes 4718600 | tf_op jit(solution)/shard_map/ppermute | solution.py:139
  89.1 5.4 %collective-permute-start.15 = (f32[384]{0:T(512)S(1)}, f32[384]{0:T(512)S(1)}, u32[]{:S(2)}, u32[]{:S(2)}) collective-permute-start(f32[384]{0:T(512)S(1)} %add.72), channel_id=1, source_target_pairs={{0,12},{2,14},{4,8},{6,10},{8,4},{10,6},{12,0},{14,2},{1,13},{3,15... | collective-permute-start | bytes 4616 | tf_op jit(solution)/shard_map/ppermute | solution.py:65
  91.7 4.5 %collective-permute-start.14 = (f32[384]{0:T(512)S(1)}, f32[384]{0:T(512)S(1)}, u32[]{:S(2)}, u32[]{:S(2)}) collective-permute-start(f32[384]{0:T(512)S(1)} %add.72), channel_id=1, source_target_pairs={{0,8},{2,10},{4,12},{6,14},{8,0},{10,2},{12,4},{14,6},{1,9},{3,11}... | collective-permute-start | bytes 4616 | tf_op jit(solution)/shard_map/ppermute | solution.py:65
  91.7 4.5 %collective-permute-start.13 = (f32[384]{0:T(512)S(1)}, f32[384]{0:T(512)S(1)}, u32[]{:S(2)}, u32[]{:S(2)}) collective-permute-start(f32[384]{0:T(512)S(1)} %add.72), channel_id=1, source_target_pairs={{0,4},{2,6},{4,0},{6,2},{8,12},{10,14},{12,8},{14,10},{1,5},{3,7},... | collective-permute-start | bytes 4616 | tf_op jit(solution)/shard_map/ppermute | solution.py:65

commit v6 on v5

--- a/solution.py
+++ b/solution.py
@@ -132,7 +132,8 @@
     out2 = narrow(own2 + wide(after(y2, passed1)))
     last = send(out2, ends)
     [own3] = products([mine(3)], fifth, out2, passed1)
-    return own3 + wide(y3) + wide(last) + wide(far0) + wide(mid1)
+    arrived = lax.optimization_barrier(own3 + wide(far0) + wide(y3))
+    return arrived + wide(last) + wide(mid1)
 
 
 def swapped(block):

time: 97.6 us -> 97.3 us (level)
  no operation moved by 1% of the time
where the time goes in v6:
time: 97.3 us; the launch traced here: 96.9 us
  Pallas kernels  40.9 us (42%)
  starting transfers between devices  28 us (29%)
  waiting for transfers between devices  16.9 us (17%)
  other arithmetic  5.09 us (5%)
  matrix products  5.07 us (5%)
    pallas_call x5, Pallas kernels, tile_products(): pl.pallas_call(kernel, out_shape=[jax.ShapeDtypeStruct((rows, n * tile),...  40.9 us
    ppermute x13, starting transfers between devices, send(): return lax.ppermute(block, 'tensor', pairs)  26.3 us
    ppermute x13, waiting for transfers between devices, send(): return lax.ppermute(block, 'tensor', pairs)  15.4 us
    dot_general x1, matrix products, reduce_line_of_four(): jnp.dot(hidden, lax.dynamic_slice_in_dim(weight, column * tile, tile, 1),...  5.07 us
    broadcast_in_dim x2, other arithmetic, per_device(): return (updated.astype(jnp.bfloat16)[None], normed[None])  2.02 us
    convert_element_type x9, other arithmetic, narrow(): return block.astype(WIRE)  1.97 us
  transfers between devices with their start and end apart: 16, of which 6 were waited for; matrix products, arithmetic and copies ran while one was open for 3% of the time, Pallas kernels for 42%

profile of v6, /device:TPU:0, one launch (start us, length us, event | category | flops | bytes accessed | tf_op | source)
XLA Modules:
  0.0 96.9 jit_solution(6984844223157347408)
XLA Ops:
  0.7 0.0 copy-start
  0.7 5.1 %fusion.6 = f16[384,512]{1,0:T(8,128)(2,1)S(1)} fusion(bf16[1,4096,8192]{2,1,0:T(8,128)(2,1)} %param.5, s32[]{:T(128)S(6)} %select_n.16, bf16[1,384,4096]{2,1,0:T(8,128)(2,1)} %param.4), kind=kOutput, calls=%fused_computation.13 | convolution fusion | flops 1610809344 | bytes 7733252 | tf_op jit(solution)/shard_map/dot_general | solution.py:103
  5.7 3.0 %collective-permute-start = (f16[384,512]{1,0:T(8,128)(2,1)S(1)}, f16[384,512]{1,0:T(8,128)(2,1)S(1)}, u32[]{:S(2)}, u32[]{:S(2)}) collective-permute-start(f16[384,512]{1,0:T(8,128)(2,1)S(1)} %fusion.6), channel_id=1, source_target_pairs={{0,2},{2,0},{4,6},{6,4},{8,10},{10,8},{12,14},{14,12},{1,3},{3,1},... | collective-permute-start | bytes 1179656 | tf_op jit(solution)/shard_map/ppermute | solution.py:65
  8.8 0.0 copy-done
  8.8 5.9 %tile_products.5 = (f32[384,512]{1,0:T(8,128)S(1)}, f32[384,512]{1,0:T(8,128)S(1)}) custom-call(s32[1]{0:T(128)} %bitcast.1.place_ref, bf16[384,4096]{1,0:T(8,128)(2,1)S(1)} %bitcast.23, bf16[4096,8192]{1,0:T(8,128)(2,1)} %bitcast.5.weight_ref), custom_call_target="tpu_custom_call" | custom-call | flops 3221225472 | bytes 9961472 | tf_op jit(solution)/shard_map/tile_products/pallas_call | solution.py:40
  14.7 0.1 convert_element_type.78
  14.8 0.1 collective-permute-start.1
  14.9 3.8 %collective-permute-done = f16[384,512]{1,0:T(8,128)(2,1)S(1)} collective-permute-done((f16[384,512]{1,0:T(8,128)(2,1)S(1)}, f16[384,512]{1,0:T(8,128)(2,1)S(1)}, u32[]{:S(2)}, u32[]{:S(2)}) %collective-permute-start) | collective-permute-done | bytes 393248 | tf_op jit(solution)/shard_map/ppermute | solution.py:65
  18.7 8.2 %tile_products.6 = (f32[384,1024]{1,0:T(8,128)S(1)}, f32[384,512]{1,0:T(8,128)S(1)}) custom-call(s32[1]{0:T(128)} %bitcast.1.place_ref, bf16[384,4096]{1,0:T(8,128)(2,1)S(1)} %bitcast.24, bf16[4096,8192]{1,0:T(8,128)(2,1)} %bitcast.5.weight_ref), custom_call_target="tpu_custom_call" | custom-call | flops 4831838208 | bytes 14942208 | tf_op jit(solution)/shard_map/tile_products/pallas_call | solution.py:40
  27.0 0.1 convert_element_type.79
  27.1 2.1 %collective-permute-start.2 = (f16[384,1024]{1,0:T(8,128)(2,1)S(1)}, f16[384,1024]{1,0:T(8,128)(2,1)S(1)}, u32[]{:S(2)}, u32[]{:S(2)}) collective-permute-start(f16[384,1024]{1,0:T(8,128)(2,1)S(1)} %convert_element_type.79), channel_id=1, source_target_pairs={{0,2},{2,0},{4,6},{6,4},{8,10},{10,8},{12,14},{14,12},{1,3},{3,1},... | collective-permute-start | bytes 2359304 | tf_op jit(solution)/shard_map/ppermute | solution.py:65
  29.2 0.0 collective-permute-done.1
  29.2 0.2 fusion.10
  29.5 3.5 %collective-permute-start.3 = (f16[384,1024]{1,0:T(8,128)(2,1)S(1)}, f16[384,1024]{1,0:T(8,128)(2,1)S(1)}, u32[]{:S(2)}, u32[]{:S(2)}) collective-permute-start(f16[384,1024]{1,0:T(8,128)(2,1)S(1)} %fusion.10), channel_id=1, source_target_pairs={{0,4},{2,6},{12,8},{14,10},{1,5},{3,7},{13,9},{15,11},{16,20},{18,... | collective-permute-start | bytes 2359304 | tf_op jit(solution)/shard_map/ppermute | solution.py:65
  33.0 10.3 %tile_products.7 = (f32[384,1024]{1,0:T(8,128)S(1)}, f32[384,1024]{1,0:T(8,128)S(1)}) custom-call(s32[1]{0:T(128)} %bitcast.1.place_ref, bf16[384,4096]{1,0:T(8,128)(2,1)S(1)} %bitcast.25, bf16[4096,8192]{1,0:T(8,128)(2,1)} %bitcast.5.weight_ref), custom_call_target="tpu_custom_call" | custom-call | flops 6442450944 | bytes 19922944 | tf_op jit(solution)/shard_map/tile_products/pallas_call | solution.py:40
  43.4 0.1 convert_element_type.82
  43.5 0.5 collective-permute-start.4
  44.0 2.7 %collective-permute-done.2 = f16[384,1024]{1,0:T(8,128)(2,1)S(1)} collective-permute-done((f16[384,1024]{1,0:T(8,128)(2,1)S(1)}, f16[384,1024]{1,0:T(8,128)(2,1)S(1)}, u32[]{:S(2)}, u32[]{:S(2)}) %collective-permute-start.2) | collective-permute-done | bytes 786464 | tf_op jit(solution)/shard_map/ppermute | solution.py:65
  46.7 0.3 fusion.9
  46.9 5.0 %collective-permute-start.5 = (f16[384,1024]{1,0:T(8,128)(2,1)S(1)}, f16[384,1024]{1,0:T(8,128)(2,1)S(1)}, u32[]{:S(2)}, u32[]{:S(2)}) collective-permute-start(f16[384,1024]{1,0:T(8,128)(2,1)S(1)} %fusion.9), channel_id=1, source_target_pairs={{0,4},{2,6},{12,8},{14,10},{1,5},{3,7},{13,9},{15,11},{16,20},{18,... | collective-permute-start | bytes 2359304 | tf_op jit(solution)/shard_map/ppermute | solution.py:65
  51.9 0.0 collective-permute-done.3
  51.9 0.4 add_convert_fusion.2
  52.3 1.3 %collective-permute-start.6 = (f16[384,1024]{1,0:T(8,128)(2,1)S(1)}, f16[384,1024]{1,0:T(8,128)(2,1)S(1)}, u32[]{:S(2)}, u32[]{:S(2)}) collective-permute-start(f16[384,1024]{1,0:T(8,128)(2,1)S(1)} %add_convert_fusion.2), channel_id=1, source_target_pairs={{4,12},{6,14},{8,0},{10,2},{5,13},{7,15},{9,1},{11,3},{20,28},{22,... | collective-permute-start | bytes 2359304 | tf_op jit(solution)/shard_map/ppermute | solution.py:65
  53.6 10.3 %tile_products.8 = (f32[384,1024]{1,0:T(8,128)S(1)}, f32[384,1024]{1,0:T(8,128)S(1)}) custom-call(s32[1]{0:T(128)} %bitcast.1.place_ref, bf16[384,4096]{1,0:T(8,128)(2,1)S(1)} %bitcast.26, bf16[4096,8192]{1,0:T(8,128)(2,1)} %bitcast.5.weight_ref), custom_call_target="tpu_custom_call" | custom-call | flops 6442450944 | bytes 19922944 | tf_op jit(solution)/shard_map/tile_products/pallas_call | solution.py:40
  63.9 0.1 convert_element_type.87
  64.1 1.7 %collective-permute-start.7 = (f16[384,1024]{1,0:T(8,128)(2,1)S(1)}, f16[384,1024]{1,0:T(8,128)(2,1)S(1)}, u32[]{:S(2)}, u32[]{:S(2)}) collective-permute-start(f16[384,1024]{1,0:T(8,128)(2,1)S(1)} %convert_element_type.87), channel_id=1, source_target_pairs={{0,2},{2,0},{4,6},{6,4},{8,10},{10,8},{12,14},{14,12},{1,3},{3,1},... | collective-permute-start | bytes 2359304 | tf_op jit(solution)/shard_map/ppermute | solution.py:65
  65.7 0.0 collective-permute-done.5
  65.7 0.4 add_convert_fusion.1
  66.2 0.0 collective-permute-done.4
  66.2 0.3 add_convert_fusion
  66.4 3.8 %collective-permute-start.8 = (f16[384,1024]{1,0:T(8,128)(2,1)S(1)}, f16[384,1024]{1,0:T(8,128)(2,1)S(1)}, u32[]{:S(2)}, u32[]{:S(2)}) collective-permute-start(f16[384,1024]{1,0:T(8,128)(2,1)S(1)} %add_convert_fusion), channel_id=1, source_target_pairs={{0,4},{2,6},{4,0},{6,2},{8,12},{10,14},{12,8},{14,10},{1,5},{3,7},... | collective-permute-start | bytes 2359304 | tf_op jit(solution)/shard_map/ppermute | solution.py:65
  70.2 0.9 collective-permute-start.9
  71.1 6.1 %tile_products.9 = f32[384,1024]{1,0:T(8,128)S(1)} custom-call(s32[1]{0:T(128)} %bitcast.1.place_ref, bf16[384,4096]{1,0:T(8,128)(2,1)S(1)} %bitcast.27, bf16[4096,8192]{1,0:T(8,128)(2,1)} %bitcast.5.weight_ref), custom_call_target="tpu_custom_call" | custom-call | flops 3221225472 | bytes 9961472 | tf_op jit(solution)/shard_map/tile_products/pallas_call | solution.py:40
  77.2 0.0 copy-start.1
  77.2 0.0 collective-permute-done.6
  77.2 1.6 %collective-permute-done.7 = f16[384,1024]{1,0:T(8,128)(2,1)S(1)} collective-permute-done((f16[384,1024]{1,0:T(8,128)(2,1)S(1)}, f16[384,1024]{1,0:T(8,128)(2,1)S(1)}, u32[]{:S(2)}, u32[]{:S(2)}) %collective-permute-start.7) | collective-permute-done | bytes 786464 | tf_op jit(solution)/shard_map/ppermute | solution.py:65
  78.8 0.4 convert_add_fusion.1
  79.2 0.0 copy-start.2
  79.2 5.8 %collective-permute-done.8 = f16[384,1024]{1,0:T(8,128)(2,1)S(1)} collective-permute-done((f16[384,1024]{1,0:T(8,128)(2,1)S(1)}, f16[384,1024]{1,0:T(8,128)(2,1)S(1)}, u32[]{:S(2)}, u32[]{:S(2)}) %collective-permute-start.8) | collective-permute-done | bytes 786464 | tf_op jit(solution)/shard_map/ppermute | solution.py:65
  85.0 0.0 collective-permute-done.9
  85.0 0.0 copy-done.1
  85.0 0.5 multiply_reduce_fusion
  85.5 0.1 collective-permute-start.11
  85.6 1.5 %collective-permute-start.10 = (f32[384]{0:T(512)S(1)}, f32[384]{0:T(512)S(1)}, u32[]{:S(2)}, u32[]{:S(2)}) collective-permute-start(f32[384]{0:T(512)S(1)} %get-tuple-element.40), channel_id=1, source_target_pairs={{0,1},{1,0},{2,3},{3,2},{4,5},{5,4},{6,7},{7,6},{8,9},{9,8},{10,11... | collective-permute-start | bytes 4616 | tf_op jit(solution)/shard_map/ppermute | solution.py:140
  87.1 0.0 copy-done.2
  87.1 1.5 %collective-permute-done.11 = f32[384]{0:T(512)S(1)} collective-permute-done((f32[384]{0:T(512)S(1)}, f32[384]{0:T(512)S(1)}, u32[]{:S(2)}, u32[]{:S(2)}) %collective-permute-start.11) | collective-permute-done | bytes 1568 | tf_op jit(solution)/shard_map/ppermute | solution.py:147
  88.6 0.0 collective-permute-done.10
  88.6 0.2 broadcast_multiply_fusion
  88.7 0.1 collective-permute-start.12
  88.8 2.5 %collective-permute-start.15 = (f32[384]{0:T(512)S(1)}, f32[384]{0:T(512)S(1)}, u32[]{:S(2)}, u32[]{:S(2)}) collective-permute-start(f32[384]{0:T(512)S(1)} %add.72), channel_id=1, source_target_pairs={{0,12},{2,14},{4,8},{6,10},{8,4},{10,6},{12,0},{14,2},{1,13},{3,15... | collective-permute-start | bytes 4616 | tf_op jit(solution)/shard_map/ppermute | solution.py:65
  91.4 0.0 collective-permute-start.14
  91.4 1.9 %collective-permute-start.13 = (f32[384]{0:T(512)S(1)}, f32[384]{0:T(512)S(1)}, u32[]{:S(2)}, u32[]{:S(2)}) collective-permute-start(f32[384]{0:T(512)S(1)} %add.72), channel_id=1, source_target_pairs={{0,4},{2,6},{4,0},{6,2},{8,12},{10,14},{12,8},{14,10},{1,5},{3,7},... | collective-permute-start | bytes 4616 | tf_op jit(solution)/shard_map/ppermute | solution.py:65
  93.3 1.0 %convert_bitcast_fusion = bf16[1,384,1024]{2,1,0:T(8,128)(2,1)} fusion(f32[384,1024]{1,0:T(8,128)S(1)} %get-tuple-element.39), kind=kLoop, calls=%fused_computation.19 | loop fusion | flops 393216 | bytes 2359296 | tf_op jit(solution)/shard_map/broadcast_in_dim | solution.py:181
  94.3 0.0 collective-permute-done.15
  94.3 1.6 %collective-permute-done.14 = f32[384]{0:T(512)S(1)} collective-permute-done((f32[384]{0:T(512)S(1)}, f32[384]{0:T(512)S(1)}, u32[]{:S(2)}, u32[]{:S(2)}) %collective-permute-start.14) | collective-permute-done | bytes 1568 | tf_op jit(solution)/shard_map/ppermute | solution.py:65
  95.9 0.0 collective-permute-done.13
  95.9 0.0 collective-permute-done.12
  95.9 1.0 %fusion.11 = bf16[1,384,1024]{2,1,0:T(8,128)(2,1)} fusion(f32[384,1024]{1,0:T(8,128)S(1)} %collective-permute-done.12, f32[384]{0:T(512)S(1)} %add_rsqrt_fusion), kind=kLoop, calls=%fused_computation.16 | loop fusion | flops 786432 | bytes 2360832 | tf_op jit(solution)/shard_map/broadcast_in_dim | solution.py:181
  (3 shorter events, 0.0 us)
Async XLA Ops:
  0.7 8.1 %copy-start = (bf16[1,384,4096]{2,1,0:T(8,128)(2,1)S(1)}, bf16[1,384,4096]{2,1,0:T(8,128)(2,1)}, u32[]{:S(2)}) copy-start(bf16[1,384,4096]{2,1,0:T(8,128)(2,1)} %param.4) | copy-start | bytes 9437188
  5.7 13.0 %collective-permute-start = (f16[384,512]{1,0:T(8,128)(2,1)S(1)}, f16[384,512]{1,0:T(8,128)(2,1)S(1)}, u32[]{:S(2)}, u32[]{:S(2)}) collective-permute-start(f16[384,512]{1,0:T(8,128)(2,1)S(1)} %fusion.6), channel_id=1, source_target_pairs={{0,2},{2,0},{4,6},{6,4},{8,10},{10,8},{12,14},{14,12},{1,3},{3,1},... | collective-permute-start | bytes 1179656 | tf_op jit(solution)/shard_map/ppermute | solution.py:65
  14.8 14.4 %collective-permute-start.1 = (f16[384,512]{1,0:T(8,128)(2,1)S(1)}, f16[384,512]{1,0:T(8,128)(2,1)S(1)}, u32[]{:S(2)}, u32[]{:S(2)}) collective-permute-start(f16[384,512]{1,0:T(8,128)(2,1)S(1)} %convert_element_type.78), channel_id=1, source_target_pairs={{0,2},{2,0},{4,6},{6,4},{8,10},{10,8},{12,14},{14,12},{1,3},{3,1},... | collective-permute-start | bytes 1179656 | tf_op jit(solution)/shard_map/ppermute | solution.py:65
  27.1 19.5 %collective-permute-start.2 = (f16[384,1024]{1,0:T(8,128)(2,1)S(1)}, f16[384,1024]{1,0:T(8,128)(2,1)S(1)}, u32[]{:S(2)}, u32[]{:S(2)}) collective-permute-start(f16[384,1024]{1,0:T(8,128)(2,1)S(1)} %convert_element_type.79), channel_id=1, source_target_pairs={{0,2},{2,0},{4,6},{6,4},{8,10},{10,8},{12,14},{14,12},{1,3},{3,1},... | collective-permute-start | bytes 2359304 | tf_op jit(solution)/shard_map/ppermute | solution.py:65
  29.5 22.4 %collective-permute-start.3 = (f16[384,1024]{1,0:T(8,128)(2,1)S(1)}, f16[384,1024]{1,0:T(8,128)(2,1)S(1)}, u32[]{:S(2)}, u32[]{:S(2)}) collective-permute-start(f16[384,1024]{1,0:T(8,128)(2,1)S(1)} %fusion.10), channel_id=1, source_target_pairs={{0,4},{2,6},{12,8},{14,10},{1,5},{3,7},{13,9},{15,11},{16,20},{18,... | collective-permute-start | bytes 2359304 | tf_op jit(solution)/shard_map/ppermute | solution.py:65
  43.5 22.7 %collective-permute-start.4 = (f16[384,1024]{1,0:T(8,128)(2,1)S(1)}, f16[384,1024]{1,0:T(8,128)(2,1)S(1)}, u32[]{:S(2)}, u32[]{:S(2)}) collective-permute-start(f16[384,1024]{1,0:T(8,128)(2,1)S(1)} %convert_element_type.82), channel_id=1, source_target_pairs={{0,2},{2,0},{4,6},{6,4},{8,10},{10,8},{12,14},{14,12},{1,3},{3,1},... | collective-permute-start | bytes 2359304 | tf_op jit(solution)/shard_map/ppermute | solution.py:65
  46.9 18.8 %collective-permute-start.5 = (f16[384,1024]{1,0:T(8,128)(2,1)S(1)}, f16[384,1024]{1,0:T(8,128)(2,1)S(1)}, u32[]{:S(2)}, u32[]{:S(2)}) collective-permute-start(f16[384,1024]{1,0:T(8,128)(2,1)S(1)} %fusion.9), channel_id=1, source_target_pairs={{0,4},{2,6},{12,8},{14,10},{1,5},{3,7},{13,9},{15,11},{16,20},{18,... | collective-permute-start | bytes 2359304 | tf_op jit(solution)/shard_map/ppermute | solution.py:65
  52.3 24.9 %collective-permute-start.6 = (f16[384,1024]{1,0:T(8,128)(2,1)S(1)}, f16[384,1024]{1,0:T(8,128)(2,1)S(1)}, u32[]{:S(2)}, u32[]{:S(2)}) collective-permute-start(f16[384,1024]{1,0:T(8,128)(2,1)S(1)} %add_convert_fusion.2), channel_id=1, source_target_pairs={{4,12},{6,14},{8,0},{10,2},{5,13},{7,15},{9,1},{11,3},{20,28},{22,... | collective-permute-start | bytes 2359304 | tf_op jit(solution)/shard_map/ppermute | solution.py:65
  64.1 14.7 %collective-permute-start.7 = (f16[384,1024]{1,0:T(8,128)(2,1)S(1)}, f16[384,1024]{1,0:T(8,128)(2,1)S(1)}, u32[]{:S(2)}, u32[]{:S(2)}) collective-permute-start(f16[384,1024]{1,0:T(8,128)(2,1)S(1)} %convert_element_type.87), channel_id=1, source_target_pairs={{0,2},{2,0},{4,6},{6,4},{8,10},{10,8},{12,14},{14,12},{1,3},{3,1},... | collective-permute-start | bytes 2359304 | tf_op jit(solution)/shard_map/ppermute | solution.py:65
  66.4 18.5 %collective-permute-start.8 = (f16[384,1024]{1,0:T(8,128)(2,1)S(1)}, f16[384,1024]{1,0:T(8,128)(2,1)S(1)}, u32[]{:S(2)}, u32[]{:S(2)}) collective-permute-start(f16[384,1024]{1,0:T(8,128)(2,1)S(1)} %add_convert_fusion), channel_id=1, source_target_pairs={{0,4},{2,6},{4,0},{6,2},{8,12},{10,14},{12,8},{14,10},{1,5},{3,7},... | collective-permute-start | bytes 2359304 | tf_op jit(solution)/shard_map/ppermute | solution.py:65
  70.2 14.8 %collective-permute-start.9 = (f16[384,1024]{1,0:T(8,128)(2,1)S(1)}, f16[384,1024]{1,0:T(8,128)(2,1)S(1)}, u32[]{:S(2)}, u32[]{:S(2)}) collective-permute-start(f16[384,1024]{1,0:T(8,128)(2,1)S(1)} %add_convert_fusion.1), channel_id=1, source_target_pairs={{4,8},{6,10},{8,4},{10,6},{5,9},{7,11},{9,5},{11,7},{20,24},{22,26... | collective-permute-start | bytes 2359304 | tf_op jit(solution)/shard_map/ppermute | solution.py:65
  77.2 7.8 %copy-start.1 = (bf16[1,384,1024]{2,1,0:T(8,128)(2,1)S(1)}, bf16[1,384,1024]{2,1,0:T(8,128)(2,1)}, u32[]{:S(2)}) copy-start(bf16[1,384,1024]{2,1,0:T(8,128)(2,1)} %param.6) | copy-start | bytes 2359300
  79.2 7.9 %copy-start.2 = (bf16[1,1024]{1,0:T(2,128)(2,1)S(1)}, bf16[1,1024]{1,0:T(2,128)(2,1)}, u32[]{:S(2)}) copy-start(bf16[1,1024]{1,0:T(2,128)(2,1)} %param.7) | copy-start | bytes 6148
  85.5 3.1 %collective-permute-start.11 = (f32[384]{0:T(512)S(1)}, f32[384]{0:T(512)S(1)}, u32[]{:S(2)}, u32[]{:S(2)}) collective-permute-start(f32[384]{0:T(512)S(1)} %get-tuple-element.40), channel_id=1, source_target_pairs={{0,3},{1,2},{2,1},{3,0},{4,7},{5,6},{6,5},{7,4},{8,11},{9,10},{10,... | collective-permute-start | bytes 4616 | tf_op jit(solution)/shard_map/ppermute | solution.py:147
  85.6 3.0 %collective-permute-start.10 = (f32[384]{0:T(512)S(1)}, f32[384]{0:T(512)S(1)}, u32[]{:S(2)}, u32[]{:S(2)}) collective-permute-start(f32[384]{0:T(512)S(1)} %get-tuple-element.40), channel_id=1, source_target_pairs={{0,1},{1,0},{2,3},{3,2},{4,5},{5,4},{6,7},{7,6},{8,9},{9,8},{10,11... | collective-permute-start | bytes 4616 | tf_op jit(solution)/shard_map/ppermute | solution.py:140
  88.7 7.1 %collective-permute-start.12 = (f32[384,1024]{1,0:T(8,128)S(1)}, f32[384,1024]{1,0:T(8,128)S(1)}, u32[]{:S(2)}, u32[]{:S(2)}) collective-permute-start(f32[384,1024]{1,0:T(8,128)S(1)} %broadcast_multiply_fusion), channel_id=1, source_target_pairs={{0,1},{1,0},{2,3},{3,2},{4,5},{5,4},{6,7},{7,6},{8,9},{9,8},{10,11... | collective-permute-start | bytes 4718600 | tf_op jit(solution)/shard_map/ppermute | solution.py:140
  88.8 5.4 %collective-permute-start.15 = (f32[384]{0:T(512)S(1)}, f32[384]{0:T(512)S(1)}, u32[]{:S(2)}, u32[]{:S(2)}) collective-permute-start(f32[384]{0:T(512)S(1)} %add.72), channel_id=1, source_target_pairs={{0,12},{2,14},{4,8},{6,10},{8,4},{10,6},{12,0},{14,2},{1,13},{3,15... | collective-permute-start | bytes 4616 | tf_op jit(solution)/shard_map/ppermute | solution.py:65
  91.4 4.5 %collective-permute-start.14 = (f32[384]{0:T(512)S(1)}, f32[384]{0:T(512)S(1)}, u32[]{:S(2)}, u32[]{:S(2)}) collective-permute-start(f32[384]{0:T(512)S(1)} %add.72), channel_id=1, source_target_pairs={{0,8},{2,10},{4,12},{6,14},{8,0},{10,2},{12,4},{14,6},{1,9},{3,11}... | collective-permute-start | bytes 4616 | tf_op jit(solution)/shard_map/ppermute | solution.py:65
  91.4 4.5 %collective-permute-start.13 = (f32[384]{0:T(512)S(1)}, f32[384]{0:T(512)S(1)}, u32[]{:S(2)}, u32[]{:S(2)}) collective-permute-start(f32[384]{0:T(512)S(1)} %add.72), channel_id=1, source_target_pairs={{0,4},{2,6},{4,0},{6,2},{8,12},{10,14},{12,8},{14,10},{1,5},{3,7},... | collective-permute-start | bytes 4616 | tf_op jit(solution)/shard_map/ppermute | solution.py:65
